TPU v7x, 32 devices: a whole 2x2x4 slice. The times are simulated.
32 devices in a mesh: ex: 16 (over z, y, x), hh: 2 (over core).
Axes of the slice: x: 2, y: 2, z: 4, core: 2. Of those that a mesh axis runs over, the one named last changes fastest.
Arguments:
- moe_input: bfloat16 [8192, 512], P('ex'), may hold values from -6 to 6
- out_grad: bfloat16 [8192, 512], P('ex'), may hold values from -6 to 6
- gate: float32 [8192], P('ex'), may hold values from 0.2 to 1
- route: int32 [8192, 1], P('ex'), may hold values from 0 to 15; in each aligned block of 512 rows (0 to 511, 512 to 1023, ...) at most 64 rows name the same one
- w_in: bfloat16 [16, 512, 2048], P('ex', None, 'hh'), may hold values from -0.25 to 0.25
- b_in: float32 [16, 2048], P('ex', 'hh'), may hold values from -3 to 3
- w_out: bfloat16 [16, 2048, 512], P('ex', 'hh'), may hold values from -0.125 to 0.125
- qkv: bfloat16 [3, 8192, 512], P(None, 'ex', 'hh'), may hold values from -8 to 8
Outputs:
- g_w_in: float32 [16, 512, 2048], P('ex', None, 'hh')
- g_b_in: float32 [16, 2048], P('ex', 'hh')
- g_w_out: float32 [16, 2048, 512], P('ex', 'hh')
- g_qkv: bfloat16 [3, 8192, 512], P(None, 'ex', 'hh')
Inputs may be any that keep to these rules, and one draw needn't show every extreme that they name: `route`: in the rows of one device no expert is named more than 64 times, a bound that some block reaches.
All inputs are finite; a program needn't handle non-finite values.
Results may differ from a plain program's by a relative error of at most 0.014.
Values may be sent and summed in bfloat16 or wider, within the bound.
A program may use at most 128 MiB of HBM per device.

v0:
```python
import jax
import jax.numpy as jnp
from jax import lax
from jax.sharding import PartitionSpec as P

HEADS = 16
CELLS = 64
WIN_T = 8
SHIFT = 4


def passed_along(block, axis, distance):
    devices = range(lax.axis_size(axis))
    route = [((i - distance) % len(devices), i) for i in devices]
    return lax.ppermute(block, axis, route)


def gelu_parts(act):
    cdf = 0.5 * (1.0 + lax.erf(act * 0.7071067811865476))
    dens = jnp.exp(-0.5 * act * act) * 0.3989422804014327
    return (act * cdf, cdf + act * dens)


def expert_terms(inputs, scaled, w_first, bias, w_second):
    act = jnp.dot(inputs, w_first, preferred_element_type=jnp.float32) + bias
    value, slope = gelu_parts(act)
    hidden = value.astype(jnp.bfloat16)
    d_hidden = jnp.einsum("sd,fd->sf", scaled, w_second, preferred_element_type=jnp.float32)
    d_pre = d_hidden * slope
    d_act = d_pre.astype(jnp.bfloat16)
    d_inputs = jnp.einsum("sf,df->sd", d_act, w_first, preferred_element_type=jnp.float32)
    g_first = jnp.einsum("sd,sf->df", inputs, d_act, preferred_element_type=jnp.float32)
    g_bias = jnp.sum(d_pre, axis=0)
    g_second = jnp.einsum("sf,sd->fd", hidden, scaled, preferred_element_type=jnp.float32)
    return (d_inputs, g_first, g_bias, g_second)


def window_grads(queries, keys, values, d_out, allowed, heads):
    rows, cols = queries.shape
    head_dim = cols // heads
    scale = head_dim ** (-0.5)
    qh = queries.reshape(rows, heads, head_dim)
    kh = keys.reshape(rows, heads, head_dim)
    vh = values.reshape(rows, heads, head_dim)
    oh = d_out.reshape(rows, heads, head_dim)
    scores = jnp.einsum("rhc,shc->hrs", qh, kh, preferred_element_type=jnp.float32) * scale
    scores = jnp.where(allowed[None], scores, -1e30)
    peak = jnp.max(scores, axis=-1, keepdims=True)
    expo = jnp.exp(scores - peak)
    probs = expo / jnp.sum(expo, axis=-1, keepdims=True)
    probs_b = probs.astype(jnp.bfloat16)
    d_probs = jnp.einsum("rhc,shc->hrs", oh, vh, preferred_element_type=jnp.float32)
    delta = jnp.sum(probs * d_probs, axis=-1, keepdims=True)
    d_scores = (probs * (d_probs - delta)).astype(jnp.bfloat16)
    d_q = (
        jnp.einsum("hrs,shc->rhc", d_scores, kh, preferred_element_type=jnp.float32) * scale
    ).astype(jnp.bfloat16)
    d_k = (
        jnp.einsum("hrs,rhc->shc", d_scores, qh, preferred_element_type=jnp.float32) * scale
    ).astype(jnp.bfloat16)
    d_v = jnp.einsum("hrs,rhc->shc", probs_b, oh, preferred_element_type=jnp.float32).astype(
        jnp.bfloat16
    )
    return jnp.stack([d_q, d_k, d_v]).reshape(3, rows, cols)


def local(moe_input, out_grad, gate, route, w_in, b_in, w_out, qkv):
    tok_rows, width = moe_input.shape
    experts = lax.axis_size("ex")
    capacity = max(2, 2 * tok_rows // experts)
    half = width // lax.axis_size("hh")
    member = lax.axis_index("hh")
    wrows = WIN_T * CELLS
    heads_here = HEADS // lax.axis_size("hh")
    lead = SHIFT
    start = (WIN_T - lead) * CELLS
    qkv_edge = passed_along(qkv, "ex", 1)
    choose = route[:, 0]
    onehot = (choose[:, None] == jnp.arange(experts, dtype=jnp.int32)[None, :]).astype(jnp.int32)
    slots = jnp.sum(jnp.cumsum(onehot, axis=0) * onehot, axis=1) - 1
    dest = choose * capacity + slots
    scaled = (gate[:, None] * out_grad.astype(jnp.float32)).astype(jnp.bfloat16)
    send_x = jnp.zeros((experts * capacity, width), jnp.bfloat16).at[dest].set(moe_input)
    send_s = jnp.zeros((experts * capacity, width), jnp.bfloat16).at[dest].set(scaled)
    send_x = send_x.reshape(experts, capacity, width)
    send_s = send_s.reshape(experts, capacity, width)
    got_x, got_s = (
        lax.all_to_all(send_x, "ex", split_axis=0, concat_axis=0, tiled=True),
        lax.all_to_all(send_s, "ex", split_axis=0, concat_axis=0, tiled=True),
    )
    got_x = got_x.reshape(experts * capacity, width)
    got_s = got_s.reshape(experts * capacity, width)
    d_inputs, g_first, g_bias, g_second = expert_terms(got_x, got_s, w_in[0], b_in[0], w_out[0])
    terms = d_inputs.reshape(experts, capacity, width)
    moved = lax.all_to_all(
        terms.astype(jnp.bfloat16), "ex", split_axis=0, concat_axis=0, tiled=True
    ).astype(terms.dtype)
    returned_rows = lax.psum_scatter(
        moved.astype(jnp.bfloat16), "hh", scatter_dimension=2, tiled=True
    )
    d_moe = returned_rows.reshape(experts * capacity, half)[dest]
    own_grad = lax.dynamic_slice_in_dim(out_grad, member * half, half, 1)
    d_heads = (own_grad.astype(jnp.float32) + d_moe.astype(jnp.float32)).astype(jnp.bfloat16)
    cot_edge = passed_along(d_heads, "ex", 1)
    window_qkv = jnp.concatenate([qkv_edge, qkv], axis=1)[:, start : start + tok_rows, :]
    window_cot = jnp.concatenate([cot_edge, d_heads], axis=0)[start : start + tok_rows]
    rows = jnp.arange(wrows, dtype=jnp.int32)
    first_slab = lax.axis_index("ex") == 0
    wrapped = (rows < lead * CELLS) & first_slab & (0 == 0)
    allowed = wrapped[:, None] == wrapped[None, :]
    pieces = window_grads(
        window_qkv[0], window_qkv[1], window_qkv[2], window_cot, allowed, heads_here
    )
    holder = jnp.zeros((3, wrows + tok_rows, half), jnp.bfloat16)
    holder = holder.at[:, start : start + tok_rows, :].set(pieces)
    borrowed = passed_along(holder[:, :wrows, :], "ex", -1)
    g_qkv = holder[:, wrows:, :].at[:, tok_rows - wrows :, :].add(borrowed)
    return (g_first[None], g_bias[None], g_second[None], g_qkv)


def solution(mesh):
    in_specs = (
        P("ex", None),
        P("ex", None),
        P("ex"),
        P("ex", None),
        P("ex", None, "hh"),
        P("ex", "hh"),
        P("ex", "hh", None),
        P(None, "ex", "hh"),
    )
    out_specs = (P("ex", None, "hh"), P("ex", "hh"), P("ex", "hh", None), P(None, "ex", "hh"))
    return jax.shard_map(local, mesh=mesh, in_specs=in_specs, out_specs=out_specs, check_vma=False)
```

profile of v0, /device:TPU:0, one launch (start us, length us, event | category | flops | bytes accessed | tf_op | source)
XLA Modules:
  0.0 192.3 jit_solution(16520022296917668566)
XLA Ops:
  10.8 4.0 %scatter_custom_fusion = bf16[1024,512]{1,0:T(8,128)(2,1)} fusion(s32[512]{0:T(512)S(1)} %bitcast.94, bf16[512,512]{1,0:T(8,128)(2,1)} %param.14, bf16[]{:T(256)} %constant.92.clone.1), kind=kCustom, calls=%fused_computation.52 | custom fusion | bytes 1049088 | tf_op jit(solution)/shard_map/scatter | solution.py:83
  14.8 8.3 %all-to-all-start = ((bf16[16,64,512]{2,1,0:T(8,128)(2,1)}), bf16[16,64,512]{2,1,0:T(8,128)(2,1)S(1)}, u32[]{:S(2)}, u32[]{:S(2)}) async-start(bf16[16,64,512]{2,1,0:T(8,128)(2,1)} %bitcast.5), calls=%async_computation | async-start | bytes 2097152 | tf_op jit(solution)/shard_map/all_to_all | solution.py:88
  23.1 4.0 %scatter_custom_fusion.1 = bf16[1024,512]{1,0:T(8,128)(2,1)} fusion(s32[512]{0:T(512)S(1)} %bitcast.95, bf16[512,512]{1,0:T(8,128)(2,1)} %param.15, f32[512]{0:T(512)} %param.16, bf16[]{:T(256)} %constant.92.clone.1), kind=kCustom, calls=%fused_computation.48 | custom fusion | flops 786432 | bytes 1574914 | tf_op jit(solution)/shard_map/scatter | solution.py:84
  27.1 20.4 %all-to-all-done = bf16[16,64,512]{2,1,0:T(8,128)(2,1)S(1)} async-done(((bf16[16,64,512]{2,1,0:T(8,128)(2,1)}), bf16[16,64,512]{2,1,0:T(8,128)(2,1)S(1)}, u32[]{:S(2)}, u32[]{:S(2)}) %all-to-all-start) | async-done | bytes 1048608 | tf_op jit(solution)/shard_map/all_to_all | solution.py:88
  47.5 5.8 %all-to-all-start.1 = ((bf16[16,64,512]{2,1,0:T(8,128)(2,1)}), bf16[16,64,512]{2,1,0:T(8,128)(2,1)S(1)}, u32[]{:S(2)}, u32[]{:S(2)}) async-start(bf16[16,64,512]{2,1,0:T(8,128)(2,1)} %bitcast.7), calls=%async_computation.1 | async-start | bytes 2097152 | tf_op jit(solution)/shard_map/all_to_all | solution.py:89
  53.4 3.2 %fusion.27 = f32[1024,1024]{1,0:T(8,128)} fusion(bf16[1024,512]{1,0:T(8,128)(2,1)S(1)} %bitcast.77, bf16[1,512,1024]{2,1,0:T(8,128)(2,1)S(1)} %copy-done), kind=kOutput, calls=%fused_computation.42 | convolution fusion | flops 1073741824 | bytes 6291456 | tf_op jit(solution)/shard_map/dot_general | solution.py:25
  56.7 19.7 %all-to-all-done.1 = bf16[16,64,512]{2,1,0:T(8,128)(2,1)S(1)} async-done(((bf16[16,64,512]{2,1,0:T(8,128)(2,1)}), bf16[16,64,512]{2,1,0:T(8,128)(2,1)S(1)}, u32[]{:S(2)}, u32[]{:S(2)}) %all-to-all-start.1) | async-done | bytes 1048608 | tf_op jit(solution)/shard_map/all_to_all | solution.py:89
  76.3 5.8 %fusion.43 = (f32[1024]{0:T(1024)}, bf16[1024,1024]{1,0:T(8,128)(2,1)S(1)}) fusion(f32[1024,1024]{1,0:T(8,128)} %fusion.27, f32[1024]{0:T(1024)S(1)} %bitcast.98, bf16[1024,512]{1,0:T(8,128)(2,1)S(1)} %bitcast.86, bf16[1,1024,512]{2,1,0:T(8,128)(2,1)} %param.20), kind=kOutput, calls=%fused_computation.73 | convolution fusion | flops 1086323712 | bytes 8396800 | tf_op jit(solution)/shard_map/sd,fd->sf/dot_general | solution.py:28
  82.2 1.3 copy-done.1
  83.5 1.3 convolution_convert_fusion
  84.8 30.7 %all_to_all.15 = bf16[16,64,512]{2,1,0:T(8,128)(2,1)} all-to-all(bf16[16,64,512]{2,1,0:T(8,128)(2,1)S(1)} %convolution_convert_fusion), channel_id=1, replica_groups=mesh['ex'=16,'hh'=2] {'ex'}, dimensions={0} | all-to-all | bytes 2097152 | tf_op jit(solution)/shard_map/all_to_all | solution.py:95
  117.1 18.8 %collective-permute-done = bf16[3,512,256]{2,1,0:T(8,128)(2,1)} collective-permute-done((bf16[3,512,256]{2,1,0:T(8,128)(2,1)}, bf16[3,512,256]{2,1,0:T(8,128)(2,1)}, u32[]{:S(2)}, u32[]{:S(2)}) %collective-permute-start) | collective-permute-done | bytes 786464 | tf_op jit(solution)/shard_map/ppermute | solution.py:15
  137.1 1.2 constant_dynamic-update-slice_fusion
  139.5 3.3 %gather_fusion = bf16[512,256]{1,0:T(8,128)(2,1)} fusion(bf16[1024,256]{1,0:T(8,128)(2,1)} %bitcast.76, s32[1024]{0:T(1024)S(1)} %pad_clamp_fusion), kind=kCustom, calls=%fused_computation | custom fusion | bytes 526336 | tf_op jit(solution)/shard_map/gather | solution.py:101
  144.1 6.1 %fusion.45 = (f32[8,512]{1,0:T(8,128)S(1)}, f32[8,512,512]{1,2,0:T(8,128)}) fusion(pred[512,512]{0,1:T(8,128)(4,1)} %broadcast_compare_fusion, bf16[512,8,32]{0,2,1:T(8,128)(2,1)S(1)} %bitcast.80, bf16[512,8,32]{0,2,1:T(8,128)(2,1)S(1)} %bitcast.82), kind=kOutput, calls=%fused_computation.75 | convolution fusion | flops 142606848 | bytes 9191424 | tf_op jit(solution)/shard_map/sub | solution.py:49
  150.2 3.9 %collective-permute-done.1 = bf16[512,256]{1,0:T(8,128)(2,1)S(1)} collective-permute-done((bf16[512,256]{1,0:T(8,128)(2,1)S(1)}, bf16[512,256]{1,0:T(8,128)(2,1)S(1)}, u32[]{:S(2)}, u32[]{:S(2)}) %collective-permute-start.1) | collective-permute-done | bytes 262176 | tf_op jit(solution)/shard_map/ppermute | solution.py:15
  154.2 4.8 %fusion.21 = bf16[8,32,512]{2,1,0:T(8,128)(2,1)S(1)} fusion(bf16[512,8,32]{0,2,1:T(8,128)(2,1)S(1)} %bitcast.90, f32[8,512,512]{1,2,0:T(8,128)} %get-tuple-element.43, f32[8,512]{1,0:T(8,128)S(1)} %get-tuple-element.42), kind=kOutput, calls=%fused_computation.38 | convolution fusion | flops 138543104 | bytes 8929280 | tf_op jit(solution)/shard_map/hrs,rhc->shc/dot_general | solution.py:61
  159.0 4.8 %multiply_reduce_fusion = (f32[8,512]{1,0:T(8,128)S(1)}, f32[8,512,512]{1,2,0:T(8,128)S(1)}) fusion(f32[8,512,512]{1,2,0:T(8,128)} %get-tuple-element.43, f32[8,512]{1,0:T(8,128)S(1)} %get-tuple-element.42, bf16[512,8,32]{0,2,1:T(8,128)(2,1)S(1)} %bitcast.91, bf16[512,8,32]{0,2,1:T(8,128)(2,1)S(1)} %bitcast.88), kind=kOutput, calls=%fused_computation.5 | convolution fusion | flops 140505088 | bytes 17334272 | tf_op jit(solution)/shard_map/rhc,shc->hrs/dot_general | solution.py:52
  164.9 2.5 %multiply_convert_fusion = bf16[8,512,512]{1,2,0:T(8,128)(2,1)S(1)} fusion(f32[8,512,512]{1,2,0:T(8,128)S(1)} %get-tuple-element.45, f32[8,512]{1,0:T(8,128)S(1)} %get-tuple-element.44, f32[8,512,512]{1,2,0:T(8,128)S(1)} %bitcast.75, f32[8,512]{1,0:T(8,128)S(1)} %get-tuple-element.42), kind=kLoop, calls=%fused_computation.4 | loop fusion | flops 8388608 | bytes 21004288 | tf_op jit(solution)/shard_map/convert_element_type | solution.py:54
  167.4 1.3 fusion.25
  170.0 1.8 collective-permute-start.2
  171.8 2.6 %convolution_bitcast_fusion = f32[1,512,1024]{2,1,0:T(8,128)} fusion(bf16[1024,512]{1,0:T(8,128)(2,1)S(1)} %bitcast.78, bf16[1024,1024]{1,0:T(8,128)(2,1)S(1)} %copy-done.2), kind=kOutput, calls=%fused_computation.32 | convolution fusion | flops 1073741824 | bytes 5242880 | tf_op jit(solution)/shard_map/sd,sf->df/dot_general | solution.py:32
  174.4 2.5 %fusion.18 = f32[1,1024,512]{2,1,0:T(8,128)} fusion(bf16[1024,512]{1,0:T(8,128)(2,1)S(1)} %bitcast.87, f32[1024,1024]{1,0:T(8,128)S(1)} %copy-done.8, f32[1024]{0:T(1024)S(1)} %bitcast.99), kind=kOutput, calls=%fused_computation.31 | convolution fusion | flops 1080033280 | bytes 7344128 | tf_op jit(solution)/shard_map/sf,sd->fd/dot_general | solution.py:34
  176.9 7.6 %collective-permute-done.2 = bf16[3,512,256]{2,1,0:T(8,128)(2,1)S(1)} collective-permute-done((bf16[3,512,256]{2,1,0:T(8,128)(2,1)S(1)}, bf16[3,512,256]{2,1,0:T(8,128)(2,1)S(1)}, u32[]{:S(2)}, u32[]{:S(2)}) %collective-permute-start.2) | collective-permute-done | bytes 786464 | tf_op jit(solution)/shard_map/ppermute | solution.py:15
  (53 shorter events, 12.3 us)
Async XLA Ops:
  7.2 46.3 %copy-start = (bf16[1,512,1024]{2,1,0:T(8,128)(2,1)S(1)}, bf16[1,512,1024]{2,1,0:T(8,128)(2,1)}, u32[]{:S(2)}) copy-start(bf16[1,512,1024]{2,1,0:T(8,128)(2,1)} %param.18) | copy-start | bytes 3145732
  14.8 32.8 %all-to-all-start = ((bf16[16,64,512]{2,1,0:T(8,128)(2,1)}), bf16[16,64,512]{2,1,0:T(8,128)(2,1)S(1)}, u32[]{:S(2)}, u32[]{:S(2)}) async-start(bf16[16,64,512]{2,1,0:T(8,128)(2,1)} %bitcast.5), calls=%async_computation | async-start | bytes 2097152 | tf_op jit(solution)/shard_map/all_to_all | solution.py:88
  47.5 28.8 %all-to-all-start.1 = ((bf16[16,64,512]{2,1,0:T(8,128)(2,1)}), bf16[16,64,512]{2,1,0:T(8,128)(2,1)S(1)}, u32[]{:S(2)}, u32[]{:S(2)}) async-start(bf16[16,64,512]{2,1,0:T(8,128)(2,1)} %bitcast.7), calls=%async_computation.1 | async-start | bytes 2097152 | tf_op jit(solution)/shard_map/all_to_all | solution.py:89
  53.4 86.1 %reduce-scatter.2.cloned.1.call-start = ((), (), s32[]{:S(2)}) async-start(), calls=%async_computation.4 | async-start | bytes 1572864 | tf_op jit(solution)/shard_map/reduce_scatter | solution.py:98
  53.4 22.9 %copy-start.7 = (f32[1,1024]{1,0:T(1,128)S(1)}, f32[1,1024]{1,0:T(1,128)}, u32[]{:S(2)}) copy-start(f32[1,1024]{1,0:T(1,128)} %param.19) | copy-start | bytes 12292
  76.3 5.8 %copy-start.4 = (bf16[16,64,512]{2,1,0:T(8,128)(2,1)}, bf16[16,64,512]{2,1,0:T(8,128)(2,1)S(1)}, u32[]{:S(2)}) copy-start(bf16[16,64,512]{2,1,0:T(8,128)(2,1)S(1)} %all-to-all-done.1) | copy-start | bytes 3145732
  82.2 1.3 copy-start.1
  115.6 20.4 %collective-permute-start = (bf16[3,512,256]{2,1,0:T(8,128)(2,1)}, bf16[3,512,256]{2,1,0:T(8,128)(2,1)}, u32[]{:S(2)}, u32[]{:S(2)}) collective-permute-start(bf16[3,512,256]{2,1,0:T(8,128)(2,1)} %param.21), channel_id=1, source_target_pairs={{30,0},{0,2},{2,4},{4,6},{6,8},{8,10},{10,12},{12,14},{14,16},{16,... | collective-permute-start | bytes 2359304 | tf_op jit(solution)/shard_map/ppermute | solution.py:15
  117.1 25.7 %copy-start.3 = (bf16[512,512]{1,0:T(8,128)(2,1)S(1)}, bf16[512,512]{1,0:T(8,128)(2,1)}, u32[]{:S(2)}) copy-start(bf16[512,512]{1,0:T(8,128)(2,1)} %param.15) | copy-start | bytes 1572868
  143.8 10.2 %collective-permute-start.1 = (bf16[512,256]{1,0:T(8,128)(2,1)S(1)}, bf16[512,256]{1,0:T(8,128)(2,1)S(1)}, u32[]{:S(2)}, u32[]{:S(2)}) collective-permute-start(bf16[512,256]{1,0:T(8,128)(2,1)S(1)} %add_convert_fusion), channel_id=1, source_target_pairs={{30,0},{0,2},{2,4},{4,6},{6,8},{8,10},{10,12},{12,14},{14,16},{16,... | collective-permute-start | bytes 786440 | tf_op jit(solution)/shard_map/ppermute | solution.py:15
  154.2 4.8 %copy-start.6 = (bf16[1,512,256]{1,2,0:T(8,128)(2,1)S(1)}, bf16[1,512,256]{1,2,0:T(8,128)(2,1)}, u32[]{:S(2)}) copy-start(bf16[1,512,256]{1,2,0:T(8,128)(2,1)} %copy.26) | copy-start | bytes 786436
  159.0 4.9 %slice-start = ((s8[8388608]{0:T(1024)(128)(4,1)}), s8[4194304]{0:T(1024)(128)(4,1)S(1)}, s32[]{:S(2)}) async-start(s8[8388608]{0:T(1024)(128)(4,1)} %bitcast.74), calls=%async_computation.5 | async-start | bytes 8388608
  159.0 5.8 %slice-start.1 = ((s8[8388608]{0:T(1024)(128)(4,1)}), s8[4194304]{0:T(1024)(128)(4,1)S(1)}, s32[]{:S(2)}) async-start(s8[8388608]{0:T(1024)(128)(4,1)} %bitcast.74), calls=%async_computation.6 | async-start | bytes 8388608
  169.8 2.0 %copy-start.2 = (bf16[1024,1024]{1,0:T(8,128)(2,1)S(1)}, bf16[1024,1024]{1,0:T(8,128)(2,1)}, u32[]{:S(2)}) copy-start(bf16[1024,1024]{1,0:T(8,128)(2,1)} %copy-done.1) | copy-start | bytes 6291460
  169.9 4.6 %copy-start.5 = (bf16[16,64,512]{2,1,0:T(8,128)(2,1)S(1)}, bf16[16,64,512]{2,1,0:T(8,128)(2,1)}, u32[]{:S(2)}) copy-start(bf16[16,64,512]{2,1,0:T(8,128)(2,1)} %copy-done.4) | copy-start | bytes 3145732
  169.9 4.6 %copy-start.8 = (f32[1024,1024]{1,0:T(8,128)S(1)}, f32[1024,1024]{1,0:T(8,128)}, u32[]{:S(2)}) copy-start(f32[1024,1024]{1,0:T(8,128)} %fusion.27) | copy-start | bytes 12582916
  170.0 14.5 %collective-permute-start.2 = (bf16[3,512,256]{2,1,0:T(8,128)(2,1)S(1)}, bf16[3,512,256]{2,1,0:T(8,128)(2,1)S(1)}, u32[]{:S(2)}, u32[]{:S(2)}) collective-permute-start(bf16[3,512,256]{2,1,0:T(8,128)(2,1)S(1)} %slice.83), channel_id=1, source_target_pairs={{2,0},{4,2},{6,4},{8,6},{10,8},{12,10},{14,12},{16,14},{18,16},{20... | collective-permute-start | bytes 2359304 | tf_op jit(solution)/shard_map/ppermute | solution.py:15
Sparse Core Ops, SparseCore 0:
  115.7 6.8 reduce-scatter.1
where the time goes:
time: 193 us; the launch traced here: 192 us
  waiting for transfers between devices  70.4 us (36%)
  matrix products  33.2 us (17%)
  blocking collectives  30.7 us (16%)
  starting transfers between devices  16.8 us (9%)
  between operations  14.3 us (7%)
  local copies, waits for them, and re-layouts  14 us (7%)
  other arithmetic  13 us (7%)
    all_to_all x1, blocking collectives, local(): lax.all_to_all(terms.astype(jnp.bfloat16), 'ex', split_axis=0, concat_axi...  30.7 us
    ppermute x3, waiting for transfers between devices, passed_along(): return lax.ppermute(block, axis, route)  30.3 us
    all_to_all x1, waiting for transfers between devices, local(): lax.all_to_all(send_x, 'ex', split_axis=0, concat_axis=0, tiled=True)  20.4 us
    all_to_all x1, waiting for transfers between devices, local(): lax.all_to_all(send_s, 'ex', split_axis=0, concat_axis=0, tiled=True)  19.7 us
    all_to_all x1, starting transfers between devices, local(): lax.all_to_all(send_x, 'ex', split_axis=0, concat_axis=0, tiled=True)  8.31 us
    sub x1, matrix products, window_grads(): expo = jnp.exp(scores - peak)  6.08 us
    dot_general x1, matrix products, expert_terms(): jnp.einsum('sd,fd->sf', scaled, w_second, preferred_element_type=jnp.floa...  5.84 us
    all_to_all x1, starting transfers between devices, local(): lax.all_to_all(send_s, 'ex', split_axis=0, concat_axis=0, tiled=True)  5.82 us
  transfers between devices with their start and end apart: 6, of which 5 were waited for; matrix products, arithmetic and copies ran while one was open for 12% of the time, Pallas kernels for 0%

commit v1 on v0

v1 whole, which is shorter than its diff:
```python
import functools
import math

import jax
import jax.numpy as jnp
from jax import lax
from jax.experimental import pallas as pl
from jax.experimental.pallas import tpu as pltpu
from jax.sharding import PartitionSpec as P

HEADS = 16
CELLS = 64
WIN_T = 8
SHIFT = 4


def passed_along(block, axis, distance):
    devices = range(lax.axis_size(axis))
    route = [((i - distance) % len(devices), i) for i in devices]
    return lax.ppermute(block, axis, route)


def gelu_parts(act):
    cdf = 0.5 * (1.0 + lax.erf(act * 0.7071067811865476))
    dens = jnp.exp(-0.5 * act * act) * 0.3989422804014327
    return (act * cdf, cdf + act * dens)


def expert_terms(inputs, scaled, w_first, bias, w_second):
    act = jnp.dot(inputs, w_first, preferred_element_type=jnp.float32) + bias
    value, slope = gelu_parts(act)
    hidden = value.astype(jnp.bfloat16)
    d_hidden = jnp.einsum("sd,fd->sf", scaled, w_second, preferred_element_type=jnp.float32)
    d_pre = d_hidden * slope
    d_act = d_pre.astype(jnp.bfloat16)
    d_inputs = jnp.einsum("sf,df->sd", d_act, w_first, preferred_element_type=jnp.float32)
    g_first = jnp.einsum("sd,sf->df", inputs, d_act, preferred_element_type=jnp.float32)
    g_bias = jnp.sum(d_pre, axis=0)
    g_second = jnp.einsum("sf,sd->fd", hidden, scaled, preferred_element_type=jnp.float32)
    return (d_inputs, g_first, g_bias, g_second)


def window_kernel(heads, bias_ref, edge_ref, own_ref, cot_edge_ref, cot_ref, back_ref, mine_ref,
                  q_t, k_t, cot_t, dq_t, dk_sum, dv_sum):
    lead = edge_ref.shape[1]
    rows, cols = q_t.shape[1], q_t.shape[0]
    head_dim = cols // heads
    scale = head_dim ** (-0.5)
    factor = scale * math.log2(math.e)
    queries = jnp.concatenate([edge_ref[0], own_ref[0, : rows - lead]], axis=0)
    keys = jnp.concatenate([edge_ref[1], own_ref[1, : rows - lead]], axis=0)
    values = jnp.concatenate([edge_ref[2], own_ref[2, : rows - lead]], axis=0)
    cot = jnp.concatenate([cot_edge_ref[...], cot_ref[: rows - lead]], axis=0)
    q_t[...] = queries.T
    k_t[...] = keys.T
    cot_t[...] = cot.T
    column = lax.broadcasted_iota(jnp.int32, (1, cols), 1)
    bias = bias_ref[0]
    for head in range(heads):
        own = (column // head_dim == head).astype(jnp.float32).astype(jnp.bfloat16)
        keys_h, values_h, queries_h, cot_h = keys * own, values * own, queries * own, cot * own
        d_k = d_v = None
        for part in range(2):
            span = slice(0, lead) if part == 0 else slice(lead, rows)
            scores = jnp.dot(keys_h, q_t[:, span], preferred_element_type=jnp.float32)
            low, high = scores[:lead], scores[lead:]
            if part == 0:
                high = high + bias
            else:
                low = low + bias
            scores = jnp.concatenate([low, high], axis=0)
            peak = jnp.max(scores, axis=0, keepdims=True)
            expo = jnp.exp2((scores - peak) * factor)
            probs = expo * (1.0 / jnp.sum(expo, axis=0, keepdims=True))
            d_probs = jnp.dot(values_h, cot_t[:, span], preferred_element_type=jnp.float32)
            delta = jnp.sum(probs * d_probs, axis=0, keepdims=True)
            d_scores = (probs * (d_probs - delta)).astype(jnp.bfloat16)
            probs_b = probs.astype(jnp.bfloat16)
            mine = slice(head * head_dim, (head + 1) * head_dim)
            dq_t[mine, span] = jnp.dot(k_t[mine, :], d_scores, preferred_element_type=jnp.float32) * scale
            more_k = jnp.dot(d_scores, queries_h[span], preferred_element_type=jnp.float32)
            more_v = jnp.dot(probs_b, cot_h[span], preferred_element_type=jnp.float32)
            d_k = more_k if d_k is None else d_k + more_k
            d_v = more_v if d_v is None else d_v + more_v
        if head == 0:
            dk_sum[...] = d_k
            dv_sum[...] = d_v
        else:
            dk_sum[...] += d_k
            dv_sum[...] += d_v
    d_q = dq_t[...].T.astype(jnp.bfloat16)
    d_k = (dk_sum[...] * scale).astype(jnp.bfloat16)
    d_v = dv_sum[...].astype(jnp.bfloat16)
    for place, grad in enumerate((d_q, d_k, d_v)):
        back_ref[place] = grad[:lead]
        mine_ref[place] = grad[lead:]


def window_grads(bias, edge, own, cot_edge, cot, heads):
    lead = edge.shape[1]
    rows, cols = cot.shape
    vmem = pl.BlockSpec(memory_space=pltpu.VMEM)
    return pl.pallas_call(
        functools.partial(window_kernel, heads),
        out_shape=(
            jax.ShapeDtypeStruct((3, lead, cols), jnp.bfloat16),
            jax.ShapeDtypeStruct((3, rows - lead, cols), jnp.bfloat16),
        ),
        in_specs=[pl.BlockSpec(memory_space=pltpu.SMEM)] + [vmem] * 4,
        out_specs=(vmem, vmem),
        scratch_shapes=[
            pltpu.VMEM((cols, rows), jnp.bfloat16),
            pltpu.VMEM((cols, rows), jnp.bfloat16),
            pltpu.VMEM((cols, rows), jnp.bfloat16),
            pltpu.VMEM((cols, rows), jnp.float32),
            pltpu.VMEM((rows, cols), jnp.float32),
            pltpu.VMEM((rows, cols), jnp.float32),
        ],
        compiler_params=pltpu.CompilerParams(vmem_limit_bytes=48 * 1024 * 1024),
        cost_estimate=pl.CostEstimate(
            flops=10 * rows * rows * cols, bytes_accessed=14 * rows * cols, transcendentals=heads * rows * rows
        ),
        name="window_grads",
    )(bias, edge, own, cot_edge, cot)


def local(moe_input, out_grad, gate, route, w_in, b_in, w_out, qkv):
    tok_rows, width = moe_input.shape
    experts = lax.axis_size("ex")
    capacity = max(2, 2 * tok_rows // experts)
    half = width // lax.axis_size("hh")
    member = lax.axis_index("hh")
    heads_here = HEADS // lax.axis_size("hh")
    lead = SHIFT * CELLS
    start = WIN_T * CELLS - lead
    qkv_edge = passed_along(qkv[:, start:], "ex", 1)
    choose = route[:, 0]
    onehot = (choose[:, None] == jnp.arange(experts, dtype=jnp.int32)[None, :]).astype(jnp.bfloat16)
    earlier = (jnp.arange(tok_rows)[:, None] > jnp.arange(tok_rows)[None, :]).astype(jnp.bfloat16)
    before = jnp.dot(earlier, onehot, preferred_element_type=jnp.float32)
    slots = jnp.sum(before * onehot.astype(jnp.float32), axis=1).astype(jnp.int32)
    dest = choose * capacity + slots
    place = (dest[None, :] == jnp.arange(experts * capacity, dtype=jnp.int32)[:, None]).astype(jnp.bfloat16)
    own_x = lax.dynamic_slice_in_dim(moe_input, member * half, half, 1)
    own_grad = lax.dynamic_slice_in_dim(out_grad, member * half, half, 1)
    own_s = (gate[:, None] * own_grad.astype(jnp.float32)).astype(jnp.bfloat16)
    tokens = jnp.concatenate([own_x, own_s], axis=1)
    send = jnp.dot(place, tokens, preferred_element_type=jnp.float32).astype(jnp.bfloat16)
    send = send.reshape(experts, capacity, 2 * half)
    got = lax.all_to_all(send, "ex", split_axis=0, concat_axis=0, tiled=True)
    got = got.reshape(experts * capacity, 2 * half)
    other = passed_along(got, "hh", 1)
    first, second = jnp.where(member == 0, got, other), jnp.where(member == 0, other, got)
    got_x = jnp.concatenate([first[:, :half], second[:, :half]], axis=1)
    got_s = jnp.concatenate([first[:, half:], second[:, half:]], axis=1)
    d_inputs, g_first, g_bias, g_second = expert_terms(got_x, got_s, w_in[0], b_in[0], w_out[0])
    kept = lax.dynamic_slice_in_dim(d_inputs, member * half, half, 1)
    given = lax.dynamic_slice_in_dim(d_inputs, (1 - member) * half, half, 1).astype(jnp.bfloat16)
    d_rows = (kept + passed_along(given, "hh", 1).astype(jnp.float32)).astype(jnp.bfloat16)
    returned = lax.all_to_all(
        d_rows.reshape(experts, capacity, half), "ex", split_axis=0, concat_axis=0, tiled=True
    ).reshape(experts * capacity, half)
    d_moe = lax.dot_general(place, returned, (((0,), (0,)), ((), ())), preferred_element_type=jnp.float32)
    d_heads = (own_grad.astype(jnp.float32) + d_moe).astype(jnp.bfloat16)
    cot_edge = passed_along(d_heads[start:], "ex", 1)
    bias = jnp.where(lax.axis_index("ex") == 0, -1e30, 0.0).astype(jnp.float32).reshape(1)
    back, mine = window_grads(bias, qkv_edge, qkv, cot_edge, d_heads, heads_here)
    g_qkv = jnp.concatenate([mine, passed_along(back, "ex", -1)], axis=1)
    return (g_first[None], g_bias[None], g_second[None], g_qkv)


def solution(mesh):
    in_specs = (
        P("ex", None),
        P("ex", None),
        P("ex"),
        P("ex", None),
        P("ex", None, "hh"),
        P("ex", "hh"),
        P("ex", "hh", None),
        P(None, "ex", "hh"),
    )
    out_specs = (P("ex", None, "hh"), P("ex", "hh"), P("ex", "hh", None), P(None, "ex", "hh"))
    return jax.shard_map(local, mesh=mesh, in_specs=in_specs, out_specs=out_specs, check_vma=False)
```

time: 193 us -> 112 us (0.58)
  waiting for transfers between devices: 70.4 us -> 36.8 us
  matrix products: 33.2 us -> 17.2 us
  between operations: 14.3 us -> 0.86 us
  local copies, waits for them, and re-layouts: 14 us -> 2.41 us
  starting transfers between devices: 16.8 us -> 6.3 us
  Pallas kernels: 0 us -> 9.81 us
  other arithmetic: 13 us -> 4.08 us
  blocking collectives: 30.7 us -> 34.5 us
    ppermute x3 -> x5, waiting for transfers between devices: 30.3 us -> 13.4 us  [passed_along(): return lax.ppermute(block, axis, route)]
    all_to_all x2 -> x1, waiting for transfers between devices: 40.1 us -> 23.4 us  [local(): lax.all_to_all(d_rows.reshape(experts, capacity, half), 'ex', split_axis=...]
    all_to_all x2 -> x1, starting transfers between devices: 14.1 us -> 4.25 us  [local(): lax.all_to_all(d_rows.reshape(experts, capacity, half), 'ex', split_axis=...]
    pallas_call x0 -> x1, Pallas kernels: none -> 9.81 us  [window_grads(): pl.pallas_call(functools.partial(window_kernel, heads), out_shape=(jax.Sh...]
    dot_general x4 -> x3, matrix products: 11.6 us -> 3.64 us  [the longest x1 1.88 us: local(): lax.dot_general(place, returned, (((0,), (0,)), ((), ())), preferred_elem...]
    sub x1 -> x0, matrix products: 6.08 us -> none  [window_grads(): expo = jnp.exp(scores - peak)]
    scatter x1 -> x0, other arithmetic: 4.02 us -> none  [local(): jnp.zeros((experts * capacity, width), jnp.bfloat16).at[dest].set(scaled)]
    scatter x1 -> x0, local copies, waits for them, and re-layouts: 3.95 us -> none  [local(): jnp.zeros((experts * capacity, width), jnp.bfloat16).at[dest].set(moe_input)]
  transfers between devices with their start and end apart: 6 -> 6, of which waited for: 5 -> 5; matrix products, arithmetic and copies ran while one was open for 12% -> 9% of each run, Pallas kernels for 0% -> 0%
where the time goes in v1:
time: 112 us
  waiting for transfers between devices  36.8 us (33%)
  blocking collectives  34.5 us (31%)
  matrix products  17.2 us (15%)
  Pallas kernels  9.81 us (9%)
  starting transfers between devices  6.3 us (6%)
  other arithmetic  4.08 us (4%)
  local copies, waits for them, and re-layouts  2.41 us (2%)
    all_to_all x1, blocking collectives, local(): got = lax.all_to_all(send, 'ex', split_axis=0, concat_axis=0, tiled=True)  34.5 us
    all_to_all x1, waiting for transfers between devices, local(): lax.all_to_all(d_rows.reshape(experts, capacity, half), 'ex', split_axis=...  23.4 us
    ppermute x5, waiting for transfers between devices, passed_along(): return lax.ppermute(block, axis, route)  13.4 us
    pallas_call x1, Pallas kernels, window_grads(): pl.pallas_call(functools.partial(window_kernel, heads), out_shape=(jax.Sh...  9.81 us
    dot_general x1, matrix products, expert_terms(): jnp.einsum('sf,sd->fd', hidden, scaled, preferred_element_type=jnp.float32)  4.99 us
    all_to_all x1, starting transfers between devices, local(): lax.all_to_all(d_rows.reshape(experts, capacity, half), 'ex', split_axis=...  4.25 us
    dot_general x1, matrix products, expert_terms(): jnp.einsum('sd,fd->sf', scaled, w_second, preferred_element_type=jnp.floa...  3.43 us
    dot_general x1, matrix products, expert_terms(): jnp.einsum('sd,sf->df', inputs, d_act, preferred_element_type=jnp.float32)  2.59 us
  transfers between devices with their start and end apart: 6, of which 5 were waited for; matrix products, arithmetic and copies ran while one was open for 9% of the time, Pallas kernels for 0%

profile of v1, /device:TPU:0, one launch (start us, length us, event | category | flops | bytes accessed | tf_op | source)
XLA Modules:
  0.0 111.9 jit_solution(7010283575821839277)
XLA Ops:
  0.7 1.1 fusion.13
  1.7 0.7 convert_add_fusion
  2.4 1.0 constant_dynamic-slice_fusion
  3.4 1.1 fusion.23
  4.5 0.7 fusion.10
  5.2 34.5 %all_to_all.10 = bf16[16,64,512]{2,1,0:T(8,128)(2,1)S(1)} all-to-all(bf16[16,64,512]{2,1,0:T(8,128)(2,1)S(1)} %bitcast.28), channel_id=1, replica_groups=mesh['ex'=16,'hh'=2] {'ex'}, dimensions={0} | all-to-all | bytes 2097152 | tf_op jit(solution)/shard_map/all_to_all | solution.py:150
  39.7 2.7 %collective-permute-done = bf16[1024,512]{1,0:T(8,128)(2,1)S(1)} collective-permute-done((bf16[1024,512]{1,0:T(8,128)(2,1)S(1)}, bf16[1024,512]{1,0:T(8,128)(2,1)S(1)}, u32[]{:S(2)}, u32[]{:S(2)}) %collective-permute-start) | collective-permute-done | bytes 1048608 | tf_op jit(solution)/shard_map/ppermute | solution.py:20
  42.3 0.3 broadcast_select_fusion.1
  42.9 1.3 %fusion.16 = f32[1024,1024]{1,0:T(8,128)S(1)} fusion(bf16[1,512,1024]{2,1,0:T(8,128)(2,1)S(1)} %copy-done, bf16[1024,256]{1,0:T(8,128)(2,1)S(1)} %get-tuple-element.16, bf16[1024,256]{1,0:T(8,128)(2,1)S(1)} %get-tuple-element.11), kind=kOutput, calls=%fused_computation.24 | convolution fusion | flops 1075838976 | bytes 6291456 | tf_op jit(solution)/shard_map/dot_general | solution.py:30
  44.2 0.4 copy-done.10
  44.6 3.4 %fusion.36 = (f32[1024]{0:T(1024)}, bf16[1024,1024]{1,0:T(8,128)(2,1)S(1)}) fusion(f32[1024,1024]{1,0:T(8,128)S(1)} %fusion.16, f32[1024]{0:T(1024)S(1)} %bitcast.31, bf16[1,1024,512]{2,1,0:T(8,128)(2,1)S(1)} %copy-done.10, bf16[1024,256]{1,0:T(8,128)(2,1)S(1)} %get-tuple-element.17, bf16[1024,256]{1,0:T(8,128)(2,1)S(1)} %get-tuple-element.10), kind=kOutput, calls=%fused_computation.54 | convolution fusion | flops 1088420864 | bytes 8396800 | tf_op jit(solution)/shard_map/sd,fd->sf/dot_general | solution.py:33
  48.1 1.3 %fusion.14 = f32[1024,512]{1,0:T(8,128)S(1)} fusion(bf16[1,512,1024]{2,1,0:T(8,128)(2,1)S(1)} %copy-done, bf16[1024,1024]{1,0:T(8,128)(2,1)S(1)} %get-tuple-element.15), kind=kOutput, calls=%fused_computation.22 | convolution fusion | flops 1073741824 | bytes 5242880 | tf_op jit(solution)/shard_map/sf,df->sd/dot_general | solution.py:36
  49.7 1.8 %collective-permute-done.2 = bf16[1024,256]{1,0:T(8,128)(2,1)S(1)} collective-permute-done((bf16[1024,256]{1,0:T(8,128)(2,1)S(1)}, bf16[1024,256]{1,0:T(8,128)(2,1)S(1)}, u32[]{:S(2)}, u32[]{:S(2)}) %collective-permute-start.2) | collective-permute-done | bytes 524320 | tf_op jit(solution)/shard_map/ppermute | solution.py:20
  51.4 1.0 add_convert_fusion
  52.5 4.3 %all-to-all-start.1 = ((bf16[16,64,256]{2,1,0:T(8,128)(2,1)}), bf16[16,64,256]{2,1,0:T(8,128)(2,1)}, u32[]{:S(2)}, u32[]{:S(2)}) async-start(bf16[16,64,256]{2,1,0:T(8,128)(2,1)} %bitcast.10), calls=%async_computation.1 | async-start | bytes 1048576 | tf_op jit(solution)/shard_map/all_to_all | solution.py:160
  56.8 1.8 %collective-permute-start.1 = (bf16[3,256,256]{2,1,0:T(8,128)(2,1)S(1)}, bf16[3,256,256]{2,1,0:T(8,128)(2,1)S(1)}, u32[]{:S(2)}, u32[]{:S(2)}) collective-permute-start(bf16[3,256,256]{2,1,0:T(8,128)(2,1)S(1)} %slice.22), channel_id=1, source_target_pairs={{30,0},{0,2},{2,4},{4,6},{6,8},{8,10},{10,12},{12,14},{14,16},{16,... | collective-permute-start | bytes 1179656 | tf_op jit(solution)/shard_map/ppermute | solution.py:20
  58.6 23.4 %all-to-all-done.1 = bf16[16,64,256]{2,1,0:T(8,128)(2,1)} async-done(((bf16[16,64,256]{2,1,0:T(8,128)(2,1)}), bf16[16,64,256]{2,1,0:T(8,128)(2,1)}, u32[]{:S(2)}, u32[]{:S(2)}) %all-to-all-start.1) | async-done | bytes 524320 | tf_op jit(solution)/shard_map/all_to_all | solution.py:160
  82.0 1.9 %fusion.12.cot_ref = bf16[512,256]{1,0:T(8,128)(2,1)S(1)} fusion(bf16[1024,256]{1,0:T(8,128)(2,1)} %bitcast.11, s32[512]{0:T(512)S(1)} %convert_add_fusion, bf16[512,512]{1,0:T(8,128)(2,1)} %param.9, s32[]{:T(128)S(6)} %select_n.25), kind=kOutput, calls=%fused_computation.17 | convolution fusion | flops 269352960 | bytes 1050628 | tf_op jit(solution)/shard_map/dot_general | solution.py:163
  83.9 0.7 slice.28
  84.6 8.8 %collective-permute-done.3.cot_edge_ref = bf16[256,256]{1,0:T(8,128)(2,1)S(1)} collective-permute-done((bf16[256,256]{1,0:T(8,128)(2,1)}, bf16[256,256]{1,0:T(8,128)(2,1)S(1)}, u32[]{:S(2)}, u32[]{:S(2)}) %collective-permute-start.3) | collective-permute-done | bytes 131104 | tf_op jit(solution)/shard_map/ppermute | solution.py:20
  93.3 9.8 %window_grads.1 = (bf16[3,256,256]{2,1,0:T(8,128)(2,1)S(1)}, bf16[3,256,256]{2,1,0:T(8,128)(2,1)S(1)}) custom-call(f32[1]{0:T(128)} %bitcast.9.bias_ref, bf16[3,256,256]{2,1,0:T(8,128)(2,1)S(1)} %collective-permute-done.1.edge_ref, bf16[3,512,256]{2,1,0:T(8,128)(2,1)S(1)} %copy-done.1, bf16[256,256]{1,0:T(8,128)(2,1)S(1)} %collective-permute-done.3.cot_edge_ref, ...), custom_call_target="tpu_custom_call" | custom-call | flops 671088640 | bytes 1835008 | tf_op jit(solution)/shard_map/window_grads/pallas_call | solution.py:103
  103.3 5.0 %fusion.9 = f32[1,1024,512]{2,1,0:T(8,128)} fusion(f32[1024,1024]{1,0:T(8,128)} %copy-done.12, f32[1024]{0:T(1024)S(1)} %bitcast.32, bf16[1024,256]{1,0:T(8,128)(2,1)S(1)} %copy-done.9, bf16[1024,256]{1,0:T(8,128)(2,1)S(1)} %copy-done.7), kind=kOutput, calls=%fused_computation.13 | convolution fusion | flops 1082130432 | bytes 7344128 | tf_op jit(solution)/shard_map/sf,sd->fd/dot_general | solution.py:39
  108.3 2.6 %convolution_bitcast_fusion = f32[1,512,1024]{2,1,0:T(8,128)} fusion(bf16[1024,1024]{1,0:T(8,128)(2,1)S(1)} %copy-done.3, bf16[1024,256]{1,0:T(8,128)(2,1)S(1)} %copy-done.5, bf16[1024,256]{1,0:T(8,128)(2,1)S(1)} %get-tuple-element.11), kind=kOutput, calls=%fused_computation.14 | convolution fusion | flops 1075838976 | bytes 5242880 | tf_op jit(solution)/shard_map/sd,sf->df/dot_general | solution.py:37
  111.0 0.9 pad_maximum_fusion.2
  (34 shorter events, 0.7 us)
Async XLA Ops:
  0.6 42.2 %copy-start = (bf16[1,512,1024]{2,1,0:T(8,128)(2,1)S(1)}, bf16[1,512,1024]{2,1,0:T(8,128)(2,1)}, u32[]{:S(2)}) copy-start(bf16[1,512,1024]{2,1,0:T(8,128)(2,1)} %param.12) | copy-start | bytes 3145732
  39.7 2.7 %collective-permute-start = (bf16[1024,512]{1,0:T(8,128)(2,1)S(1)}, bf16[1024,512]{1,0:T(8,128)(2,1)S(1)}, u32[]{:S(2)}, u32[]{:S(2)}) collective-permute-start(bf16[1024,512]{1,0:T(8,128)(2,1)S(1)} %bitcast.27), channel_id=1, source_target_pairs={{1,0},{0,1},{3,2},{2,3},{5,4},{4,5},{7,6},{6,7},{9,8},{8,9},{11,10... | collective-permute-start | bytes 3145736 | tf_op jit(solution)/shard_map/ppermute | solution.py:20
  42.8 1.3 %copy-start.4 = (bf16[1024,256]{1,0:T(8,128)(2,1)}, bf16[1024,256]{1,0:T(8,128)(2,1)S(1)}, u32[]{:S(2)}) copy-start(bf16[1024,256]{1,0:T(8,128)(2,1)S(1)} %get-tuple-element.16) | copy-start | bytes 1572868
  42.8 1.3 %copy-start.6 = (bf16[1024,256]{1,0:T(8,128)(2,1)}, bf16[1024,256]{1,0:T(8,128)(2,1)S(1)}, u32[]{:S(2)}) copy-start(bf16[1024,256]{1,0:T(8,128)(2,1)S(1)} %get-tuple-element.10) | copy-start | bytes 1572868
  42.8 1.3 %copy-start.8 = (bf16[1024,256]{1,0:T(8,128)(2,1)}, bf16[1024,256]{1,0:T(8,128)(2,1)S(1)}, u32[]{:S(2)}) copy-start(bf16[1024,256]{1,0:T(8,128)(2,1)S(1)} %get-tuple-element.17) | copy-start | bytes 1572868
  42.9 1.8 %copy-start.10 = (bf16[1,1024,512]{2,1,0:T(8,128)(2,1)S(1)}, bf16[1,1024,512]{2,1,0:T(8,128)(2,1)}, u32[]{:S(2)}) copy-start(bf16[1,1024,512]{2,1,0:T(8,128)(2,1)} %param.14) | copy-start | bytes 3145732
  42.9 1.8 %copy-start.11 = (f32[1,1024]{1,0:T(1,128)S(1)}, f32[1,1024]{1,0:T(1,128)}, u32[]{:S(2)}) copy-start(f32[1,1024]{1,0:T(1,128)} %param.13) | copy-start | bytes 12292
  44.2 3.9 %copy-start.12 = (f32[1024,1024]{1,0:T(8,128)}, f32[1024,1024]{1,0:T(8,128)S(1)}, u32[]{:S(2)}) copy-start(f32[1024,1024]{1,0:T(8,128)S(1)} %fusion.16) | copy-start | bytes 12582916
  48.1 1.3 %copy-start.2 = (bf16[1024,1024]{1,0:T(8,128)(2,1)}, bf16[1024,1024]{1,0:T(8,128)(2,1)S(1)}, u32[]{:S(2)}) copy-start(bf16[1024,1024]{1,0:T(8,128)(2,1)S(1)} %get-tuple-element.15) | copy-start | bytes 6291460
  49.4 7.3 %copy-start.1 = (bf16[3,512,256]{2,1,0:T(8,128)(2,1)S(1)}, bf16[3,512,256]{2,1,0:T(8,128)(2,1)}, u32[]{:S(2)}) copy-start(bf16[3,512,256]{2,1,0:T(8,128)(2,1)} %own_ref.1) | copy-start | bytes 2359300
  49.5 2.0 %collective-permute-start.2 = (bf16[1024,256]{1,0:T(8,128)(2,1)S(1)}, bf16[1024,256]{1,0:T(8,128)(2,1)S(1)}, u32[]{:S(2)}, u32[]{:S(2)}) collective-permute-start(bf16[1024,256]{1,0:T(8,128)(2,1)S(1)} %dynamic-slice_convert_fusion), channel_id=1, source_target_pairs={{1,0},{0,1},{3,2},{2,3},{5,4},{4,5},{7,6},{6,7},{9,8},{8,9},{11,10... | collective-permute-start | bytes 1572872 | tf_op jit(solution)/shard_map/ppermute | solution.py:20
  52.5 29.5 %all-to-all-start.1 = ((bf16[16,64,256]{2,1,0:T(8,128)(2,1)}), bf16[16,64,256]{2,1,0:T(8,128)(2,1)}, u32[]{:S(2)}, u32[]{:S(2)}) async-start(bf16[16,64,256]{2,1,0:T(8,128)(2,1)} %bitcast.10), calls=%async_computation.1 | async-start | bytes 1048576 | tf_op jit(solution)/shard_map/all_to_all | solution.py:160
  56.8 27.8 %collective-permute-start.1 = (bf16[3,256,256]{2,1,0:T(8,128)(2,1)S(1)}, bf16[3,256,256]{2,1,0:T(8,128)(2,1)S(1)}, u32[]{:S(2)}, u32[]{:S(2)}) collective-permute-start(bf16[3,256,256]{2,1,0:T(8,128)(2,1)S(1)} %slice.22), channel_id=1, source_target_pairs={{30,0},{0,2},{2,4},{4,6},{6,8},{8,10},{10,12},{12,14},{14,16},{16,... | collective-permute-start | bytes 1179656 | tf_op jit(solution)/shard_map/ppermute | solution.py:20
  84.6 8.8 %collective-permute-start.3 = (bf16[256,256]{1,0:T(8,128)(2,1)}, bf16[256,256]{1,0:T(8,128)(2,1)S(1)}, u32[]{:S(2)}, u32[]{:S(2)}) collective-permute-start(bf16[256,256]{1,0:T(8,128)(2,1)} %slice.28), channel_id=1, source_target_pairs={{30,0},{0,2},{2,4},{4,6},{6,8},{8,10},{10,12},{12,14},{14,16},{16,... | collective-permute-start | bytes 393224 | tf_op jit(solution)/shard_map/ppermute | solution.py:20
  84.6 18.7 %copy-start.7 = (bf16[1024,256]{1,0:T(8,128)(2,1)S(1)}, bf16[1024,256]{1,0:T(8,128)(2,1)}, u32[]{:S(2)}) copy-start(bf16[1024,256]{1,0:T(8,128)(2,1)} %copy-done.6) | copy-start | bytes 1572868
  84.6 18.7 %copy-start.9 = (bf16[1024,256]{1,0:T(8,128)(2,1)S(1)}, bf16[1024,256]{1,0:T(8,128)(2,1)}, u32[]{:S(2)}) copy-start(bf16[1024,256]{1,0:T(8,128)(2,1)} %copy-done.8) | copy-start | bytes 1572868
  103.1 5.1 %copy-start.3 = (bf16[1024,1024]{1,0:T(8,128)(2,1)S(1)}, bf16[1024,1024]{1,0:T(8,128)(2,1)}, u32[]{:S(2)}) copy-start(bf16[1024,1024]{1,0:T(8,128)(2,1)} %copy-done.2) | copy-start | bytes 6291460
  103.2 5.1 %copy-start.5 = (bf16[1024,256]{1,0:T(8,128)(2,1)S(1)}, bf16[1024,256]{1,0:T(8,128)(2,1)}, u32[]{:S(2)}) copy-start(bf16[1024,256]{1,0:T(8,128)(2,1)} %copy-done.4) | copy-start | bytes 1572868
  103.2 7.8 %collective-permute-start.4 = (bf16[3,256,256]{2,1,0:T(8,128)(2,1)S(1)}, bf16[3,256,256]{2,1,0:T(8,128)(2,1)S(1)}, u32[]{:S(2)}, u32[]{:S(2)}) collective-permute-start(bf16[3,256,256]{2,1,0:T(8,128)(2,1)S(1)} %get-tuple-element.7), channel_id=1, source_target_pairs={{2,0},{4,2},{6,4},{8,6},{10,8},{12,10},{14,12},{16,14},{18,16},{20... | collective-permute-start | bytes 1179656 | tf_op jit(solution)/shard_map/ppermute | solution.py:20

commit v2 on v1

--- a/solution.py
+++ b/solution.py
@@ -123,6 +123,201 @@
         name="window_grads",
     )(bias, edge, own, cot_edge, cot)
 
+MESH = pl.DeviceIdType.MESH
+
+
+def exchange_kernel(n, group, send_ref, qkv_ref, w_in_ref, b_ref, w_out_ref, place_t_ref, grad_ref,
+                    got_ref, dact_ref, hidden_ref, gb_ref, edge_ref, cot_edge_ref, heads_ref,
+                    w_in_t, w_out_t, part_out, part_in, ret_out, ret_in,
+                    send_sem, recv_sem, on_send, on_recv, part_send, part_recv, ret_send, ret_recv,
+                    edge_sem, cot_sem, own_sem):
+    me, core = lax.axis_index("ex"), lax.axis_index("hh")
+    after, sibling = lax.rem(me + 1, n), 1 - core
+    capacity, half = ret_in.shape[1], ret_in.shape[2]
+    rows = group * capacity
+    lead = edge_ref.shape[1]
+    start = qkv_ref.shape[1] - lead
+    hidden_units = w_in_ref.shape[1]
+    bits = n.bit_length() - 1
+
+    def partner(k):
+        total = 0
+        for b in range(bits):
+            bit = lax.rem(lax.div(me, 1 << b), 2)
+            total = total + ((1 - bit) if (k >> b) & 1 else bit) * (1 << b)
+        return total
+
+    partners = [partner(k) for k in range(n)]
+    barrier = pltpu.get_barrier_semaphore()
+    for k in range(1, n):
+        pl.semaphore_signal(barrier, inc=1, device_id=(partners[k], core), device_id_type=MESH)
+    pl.semaphore_signal(barrier, inc=1, device_id=(me, sibling), device_id_type=MESH)
+    pl.semaphore_wait(barrier, n)
+
+    def remote(src, dst, send, recv, device):
+        return pltpu.make_async_remote_copy(
+            src_ref=src, dst_ref=dst, send_sem=send, recv_sem=recv, device_id=device, device_id_type=MESH
+        )
+
+    out = {
+        k: remote(send_ref.at[partners[k]], got_ref.at[core, me], send_sem.at[k], recv_sem.at[k],
+                  (partners[k], core))
+        for k in range(1, n)
+    }
+    passed = {
+        k: remote(got_ref.at[core, partners[k]], got_ref.at[core, partners[k]], on_send.at[k], on_recv.at[k],
+                  (me, sibling))
+        for k in range(n)
+    }
+    far = list(range(n // 2, n))
+    near = list(range(1, n // 2))
+    order = []
+    while far or near:
+        order += far[:2] + near[:1]
+        far, near = far[2:], near[1:]
+    for k in order:
+        out[k].start()
+    own = pltpu.make_async_copy(send_ref.at[me], got_ref.at[core, me], own_sem.at[0])
+    own.start()
+    edge = remote(qkv_ref.at[:, pl.ds(start, lead)], edge_ref, edge_sem.at[0], edge_sem.at[1], (after, core))
+    edge.start()
+    w_in_t[...] = w_in_ref[...].T
+    w_out_t[...] = w_out_ref[...].T
+
+    back = {}
+    parts = []
+    step = hidden_units // 4
+    bias_sums = [0.0] * 4
+    for g in range(n // group):
+        ks = range(g * group, (g + 1) * group)
+        for k in ks:
+            if k == 0:
+                own.wait()
+            else:
+                out[k].wait_recv()
+            passed[k].start()
+        for k in ks:
+            passed[k].wait_recv()
+        base = lax.div(partners[g * group], group) * group
+        low = got_ref[0, pl.ds(base, group)].reshape(rows, 2 * half)
+        high = got_ref[1, pl.ds(base, group)].reshape(rows, 2 * half)
+        x = jnp.concatenate([low[:, :half], high[:, :half]], axis=1)
+        s = jnp.concatenate([low[:, half:], high[:, half:]], axis=1)
+        span = pl.ds(pl.multiple_of(base * capacity, rows), rows)
+        d_rows = None
+        for c in range(4):
+            cols = slice(c * step, (c + 1) * step)
+            act = jnp.dot(x, w_in_ref[:, cols], preferred_element_type=jnp.float32) + b_ref[:, cols]
+            value, slope = gelu_parts(act)
+            hidden_ref[span, cols] = value.astype(jnp.bfloat16)
+            d_pre = jnp.dot(s, w_out_t[:, cols], preferred_element_type=jnp.float32) * slope
+            d_act = d_pre.astype(jnp.bfloat16)
+            dact_ref[span, cols] = d_act
+            bias_sums[c] = bias_sums[c] + jnp.sum(d_pre, axis=0, keepdims=True)
+            more = jnp.dot(d_act, w_in_t[cols, :], preferred_element_type=jnp.float32)
+            d_rows = more if d_rows is None else d_rows + more
+        kept = jnp.where(core == 0, d_rows[:, :half], d_rows[:, half:])
+        given = jnp.where(core == 0, d_rows[:, half:], d_rows[:, :half])
+        part_out[g] = given.astype(jnp.bfloat16)
+        swap = remote(part_out.at[g], part_in.at[g], part_send.at[g], part_recv.at[g], (me, sibling))
+        swap.start()
+        parts.append(swap)
+        swap.wait_recv()
+        total = (kept + part_in[g].astype(jnp.float32)).astype(jnp.bfloat16)
+        ret_out[pl.ds(base, group)] = total.reshape(group, capacity, half)
+        for k in reversed(ks):
+            if k == 0:
+                back[k] = pltpu.make_async_copy(ret_out.at[me], ret_in.at[me], own_sem.at[1])
+            else:
+                back[k] = remote(ret_out.at[partners[k]], ret_in.at[me], ret_send.at[k], ret_recv.at[k],
+                                 (partners[k], core))
+            back[k].start()
+    for c in range(4):
+        gb_ref[:, c * step : (c + 1) * step] = bias_sums[c]
+
+    total = grad_ref[...].astype(jnp.float32)
+    for g in range(n // group):
+        for k in range(g * group, (g + 1) * group):
+            if k == 0:
+                back[k].wait()
+            else:
+                back[k].wait_recv()
+        base = lax.div(partners[g * group], group) * group
+        span = pl.ds(pl.multiple_of(base * capacity, rows), rows)
+        total = total + jnp.dot(
+            place_t_ref[:, span], ret_in[pl.ds(base, group)].reshape(rows, half),
+            preferred_element_type=jnp.float32,
+        )
+    heads_ref[...] = total.astype(jnp.bfloat16)
+    cot = remote(heads_ref.at[pl.ds(start, lead)], cot_edge_ref, cot_sem.at[0], cot_sem.at[1], (after, core))
+    cot.start()
+    for k in range(n):
+        passed[k].wait_send()
+        if k > 0:
+            out[k].wait_send()
+            back[k].wait_send()
+    for swap in parts:
+        swap.wait_send()
+    edge.wait()
+    cot.wait()
+
+
+def exchange(send, qkv, w_in, b_in, w_out, place_t, own_grad, lead):
+    n, capacity, columns = send.shape
+    half = columns // 2
+    width, hidden_units = w_in.shape
+    group = 4
+    vmem = pl.BlockSpec(memory_space=pltpu.VMEM)
+    bf16, f32 = jnp.bfloat16, jnp.float32
+    dma = pltpu.SemaphoreType.DMA
+    shape = jax.ShapeDtypeStruct
+    return pl.pallas_call(
+        functools.partial(exchange_kernel, n, group),
+        out_shape=(
+            shape((2, n, capacity, columns), bf16),
+            shape((n * capacity, hidden_units), bf16),
+            shape((n * capacity, hidden_units), bf16),
+            shape((1, hidden_units), f32),
+            shape((3, lead, half), bf16),
+            shape((lead, half), bf16),
+            shape(own_grad.shape, bf16),
+        ),
+        in_specs=[vmem] * 7,
+        out_specs=[vmem] * 7,
+        scratch_shapes=[
+            pltpu.VMEM((hidden_units, width), bf16),
+            pltpu.VMEM((width, hidden_units), bf16),
+            pltpu.VMEM((n // group, group * capacity, half), bf16),
+            pltpu.VMEM((n // group, group * capacity, half), bf16),
+            pltpu.VMEM((n, capacity, half), bf16),
+            pltpu.VMEM((n, capacity, half), bf16),
+            dma((n,)), dma((n,)), dma((n,)), dma((n,)),
+            dma((n // group,)), dma((n // group,)),
+            dma((n,)), dma((n,)),
+            dma((2,)), dma((2,)), dma((2,)),
+        ],
+        compiler_params=pltpu.CompilerParams(
+            collective_id=0, has_side_effects=True, vmem_limit_bytes=48 * 1024 * 1024
+        ),
+        cost_estimate=pl.CostEstimate(
+            flops=6 * n * capacity * width * hidden_units, bytes_accessed=16 * 1024 * 1024,
+            transcendentals=2 * n * capacity * hidden_units,
+        ),
+        name="exchange",
+    )(send, qkv, w_in, b_in, w_out, place_t, own_grad)
+
+
+def weight_grads(x, s, d_act, hidden):
+    g_first = jnp.einsum("sd,sf->df", x, d_act, preferred_element_type=jnp.float32)
+    g_second = jnp.einsum("sf,sd->fd", hidden, s, preferred_element_type=jnp.float32)
+    return g_first, g_second
+
+
+def columns_joined(low, high, half):
+    x = jnp.concatenate([low[:, :half], high[:, :half]], axis=1)
+    s = jnp.concatenate([low[:, half:], high[:, half:]], axis=1)
+    return x, s
+
 
 def local(moe_input, out_grad, gate, route, w_in, b_in, w_out, qkv):
     tok_rows, width = moe_input.shape
@@ -133,7 +328,6 @@
     heads_here = HEADS // lax.axis_size("hh")
     lead = SHIFT * CELLS
     start = WIN_T * CELLS - lead
-    qkv_edge = passed_along(qkv[:, start:], "ex", 1)
     choose = route[:, 0]
     onehot = (choose[:, None] == jnp.arange(experts, dtype=jnp.int32)[None, :]).astype(jnp.bfloat16)
     earlier = (jnp.arange(tok_rows)[:, None] > jnp.arange(tok_rows)[None, :]).astype(jnp.bfloat16)
@@ -147,22 +341,31 @@
     tokens = jnp.concatenate([own_x, own_s], axis=1)
     send = jnp.dot(place, tokens, preferred_element_type=jnp.float32).astype(jnp.bfloat16)
     send = send.reshape(experts, capacity, 2 * half)
-    got = lax.all_to_all(send, "ex", split_axis=0, concat_axis=0, tiled=True)
-    got = got.reshape(experts * capacity, 2 * half)
-    other = passed_along(got, "hh", 1)
-    first, second = jnp.where(member == 0, got, other), jnp.where(member == 0, other, got)
-    got_x = jnp.concatenate([first[:, :half], second[:, :half]], axis=1)
-    got_s = jnp.concatenate([first[:, half:], second[:, half:]], axis=1)
-    d_inputs, g_first, g_bias, g_second = expert_terms(got_x, got_s, w_in[0], b_in[0], w_out[0])
-    kept = lax.dynamic_slice_in_dim(d_inputs, member * half, half, 1)
-    given = lax.dynamic_slice_in_dim(d_inputs, (1 - member) * half, half, 1).astype(jnp.bfloat16)
-    d_rows = (kept + passed_along(given, "hh", 1).astype(jnp.float32)).astype(jnp.bfloat16)
-    returned = lax.all_to_all(
-        d_rows.reshape(experts, capacity, half), "ex", split_axis=0, concat_axis=0, tiled=True
-    ).reshape(experts * capacity, half)
-    d_moe = lax.dot_general(place, returned, (((0,), (0,)), ((), ())), preferred_element_type=jnp.float32)
-    d_heads = (own_grad.astype(jnp.float32) + d_moe).astype(jnp.bfloat16)
-    cot_edge = passed_along(d_heads[start:], "ex", 1)
+    if capacity % 16 == 0 and experts % 4 == 0 and experts & (experts - 1) == 0:
+        got, d_act, hidden, g_bias, qkv_edge, cot_edge, d_heads = exchange(
+            send, qkv, w_in[0], b_in, w_out[0], place.T, own_grad, lead
+        )
+        g_bias = g_bias[0]
+        got = got.reshape(2, experts * capacity, 2 * half)
+        got_x, got_s = columns_joined(got[0], got[1], half)
+        g_first, g_second = weight_grads(got_x, got_s, d_act, hidden)
+    else:
+        qkv_edge = passed_along(qkv[:, start:], "ex", 1)
+        got = lax.all_to_all(send, "ex", split_axis=0, concat_axis=0, tiled=True)
+        got = got.reshape(experts * capacity, 2 * half)
+        other = passed_along(got, "hh", 1)
+        first, second = jnp.where(member == 0, got, other), jnp.where(member == 0, other, got)
+        got_x, got_s = columns_joined(first, second, half)
+        d_inputs, g_first, g_bias, g_second = expert_terms(got_x, got_s, w_in[0], b_in[0], w_out[0])
+        kept = lax.dynamic_slice_in_dim(d_inputs, member * half, half, 1)
+        given = lax.dynamic_slice_in_dim(d_inputs, (1 - member) * half, half, 1).astype(jnp.bfloat16)
+        d_rows = (kept + passed_along(given, "hh", 1).astype(jnp.float32)).astype(jnp.bfloat16)
+        returned = lax.all_to_all(
+            d_rows.reshape(experts, capacity, half), "ex", split_axis=0, concat_axis=0, tiled=True
+        ).reshape(experts * capacity, half)
+        d_moe = lax.dot_general(place, returned, (((0,), (0,)), ((), ())), preferred_element_type=jnp.float32)
+        d_heads = (own_grad.astype(jnp.float32) + d_moe).astype(jnp.bfloat16)
+        cot_edge = passed_along(d_heads[start:], "ex", 1)
     bias = jnp.where(lax.axis_index("ex") == 0, -1e30, 0.0).astype(jnp.float32).reshape(1)
     back, mine = window_grads(bias, qkv_edge, qkv, cot_edge, d_heads, heads_here)
     g_qkv = jnp.concatenate([mine, passed_along(back, "ex", -1)], axis=1)

time: 112 us -> 88.1 us (0.79)
  Pallas kernels: 9.81 us -> 69.1 us
  waiting for transfers between devices: 36.8 us -> 0.21 us
  blocking collectives: 34.5 us -> 0 us
  matrix products: 17.2 us -> 7.9 us
  starting transfers between devices: 6.3 us -> 0.81 us
  local copies, waits for them, and re-layouts: 2.41 us -> 5.97 us
    pallas_call x0 -> x1, Pallas kernels: none -> 59 us  [exchange(): pl.pallas_call(functools.partial(exchange_kernel, n, group), out_shape=(s...]
    all_to_all x1 -> x0, blocking collectives: 34.5 us -> none  [local(): got = lax.all_to_all(send, 'ex', split_axis=0, concat_axis=0, tiled=True)]
    all_to_all x1 -> x0, waiting for transfers between devices: 23.4 us -> none  [local(): lax.all_to_all(d_rows.reshape(experts, capacity, half), 'ex', split_axis=...]
    ppermute x5 -> x1, waiting for transfers between devices: 13.4 us -> 0.21 us  [passed_along(): return lax.ppermute(block, axis, route)]
    dot_general x6 -> x2, matrix products: 15.4 us -> 5.19 us  [the longest x1 2.6 us: weight_grads(): jnp.einsum('sf,sd->fd', hidden, s, preferred_element_type=jnp.float32)]
    unnamed x26 -> x21, local copies, waits for them, and re-layouts: 0.54 us -> 5.65 us
    all_to_all x1 -> x0, starting transfers between devices: 4.25 us -> none  [local(): lax.all_to_all(d_rows.reshape(experts, capacity, half), 'ex', split_axis=...]
    ppermute x5 -> x1, starting transfers between devices: 2.05 us -> 0.81 us  [passed_along(): return lax.ppermute(block, axis, route)]
  transfers between devices with their start and end apart: 6 -> 1, of which waited for: 5 -> 1; matrix products, arithmetic and copies ran while one was open for 9% -> 6% of each run, Pallas kernels for 0% -> 0%
where the time goes in v2:
time: 88.1 us; the launch traced here: 87.7 us
  Pallas kernels  69.1 us (78%)
  matrix products  7.9 us (9%)
  local copies, waits for them, and re-layouts  5.97 us (7%)
  other arithmetic  3.04 us (3%)
    pallas_call x1, Pallas kernels, exchange(): pl.pallas_call(functools.partial(exchange_kernel, n, group), out_shape=(s...  59 us
    pallas_call x1, Pallas kernels, window_grads(): pl.pallas_call(functools.partial(window_kernel, heads), out_shape=(jax.Sh...  10 us
    unnamed x21, local copies, waits for them, and re-layouts  5.65 us
    dot_general x1, matrix products, weight_grads(): jnp.einsum('sf,sd->fd', hidden, s, preferred_element_type=jnp.float32)  2.6 us
    dot_general x1, matrix products, weight_grads(): jnp.einsum('sd,sf->df', x, d_act, preferred_element_type=jnp.float32)  2.6 us
  transfers between devices with their start and end apart: 1, of which 1 were waited for; matrix products, arithmetic and copies ran while one was open for 6% of the time, Pallas kernels for 0%

profile of v2, /device:TPU:0, one launch (start us, length us, event | category | flops | bytes accessed | tf_op | source)
XLA Modules:
  0.0 87.7 jit_solution(899837710299186287)
XLA Ops:
  0.6 0.0 copy-start
  0.7 1.0 %fusion.3 = f32[512]{0:T(512)S(1)} fusion(s32[512]{0:T(512)} %bitcast.18), kind=kOutput, calls=%fused_computation.8 | convolution fusion | flops 8699392 | bytes 4096 | tf_op jit(solution)/shard_map/dot_general | solution.py:334
  1.7 0.7 convert_add_fusion
  2.4 0.2 fusion.1.place_t_ref
  2.6 0.0 copy-done
  2.6 0.0 copy-start.1
  2.6 0.0 copy-start.5
  2.7 1.2 %multiply_convert_fusion = (bf16[512,256]{1,0:T(8,128)(2,1)S(1)}, bf16[512,256]{1,0:T(8,128)(2,1)S(1)}) fusion(f32[512]{0:T(512)} %param.10, bf16[512,512]{1,0:T(8,128)(2,1)} %param.9, s32[]{:T(128)S(6)} %select_n.8), kind=kLoop, calls=%fused_computation.21 | loop fusion | flops 393216 | bytes 788484 | tf_op jit(solution)/shard_map/convert_element_type | solution.py:340
  3.9 1.7 %fusion.2 = bf16[1024,512]{1,0:T(8,128)(2,1)} fusion(s32[512]{0:T(512)S(1)} %convert_add_fusion, bf16[512,256]{1,0:T(8,128)(2,1)S(1)} %get-tuple-element.22, bf16[512,256]{1,0:T(8,128)(2,1)S(1)} %constant_dynamic-slice_fusion.1), kind=kOutput, calls=%fused_computation.6 | convolution fusion | flops 538968064 | bytes 1574912 | tf_op jit(solution)/shard_map/dot_general | solution.py:342
  5.6 0.0 copy-done.1
  5.6 1.2 %copy-done.2 = bf16[1,1024,512]{2,1,0:T(8,128)(2,1)S(1)} copy-done((bf16[1,1024,512]{2,1,0:T(8,128)(2,1)S(1)}, bf16[1,1024,512]{2,1,0:T(8,128)(2,1)}, u32[]{:S(2)}) %copy-start.2) | copy-done | bytes 1048600
  6.8 1.1 %copy-done.3 = bf16[3,512,256]{2,1,0:T(8,128)(2,1)S(1)} copy-done((bf16[3,512,256]{2,1,0:T(8,128)(2,1)S(1)}, bf16[3,512,256]{2,1,0:T(8,128)(2,1)}, u32[]{:S(2)}) %copy-start.3) | copy-done | bytes 786456
  7.9 1.2 %copy-done.6 = bf16[1024,512]{1,0:T(8,128)(2,1)S(1)} copy-done((bf16[1024,512]{1,0:T(8,128)(2,1)S(1)}, bf16[1024,512]{1,0:T(8,128)(2,1)}, u32[]{:S(2)}) %copy-start.6) | copy-done | bytes 1048600
  9.2 59.0 %exchange.1 = (bf16[2,16,64,512]{3,2,1,0:T(8,128)(2,1)}, bf16[1024,1024]{1,0:T(8,128)(2,1)}, bf16[1024,1024]{1,0:T(8,128)(2,1)}, f32[1,1024]{1,0:T(1,128)S(1)}, ...) custom-call(bf16[16,64,512]{2,1,0:T(8,128)(2,1)S(1)} %bitcast.15, ...), custom_call_target="tpu_custom_call" | custom-call | flops 3221225472 | bytes 16777216 | tf_op jit(solution)/shard_map/exchange/pallas_call | solution.py:274
  68.2 10.0 %window_grads.1 = (bf16[3,256,256]{2,1,0:T(8,128)(2,1)S(1)}, bf16[3,256,256]{2,1,0:T(8,128)(2,1)S(1)}) custom-call(f32[1]{0:T(128)} %bitcast.8.bias_ref, bf16[3,256,256]{2,1,0:T(8,128)(2,1)S(1)} %get-tuple-element.17.edge_ref, bf16[3,512,256]{2,1,0:T(8,128)(2,1)S(1)} %copy-done.4, bf16[256,256]{1,0:T(8,128)(2,1)S(1)} %get-tuple-element.18.cot_edge_ref, ...), custom_call_target="tpu_custom_call" | custom-call | flops 671088640 | bytes 1835008 | tf_op jit(solution)/shard_map/window_grads/pallas_call | solution.py:103
  78.2 0.8 collective-permute-start
  79.1 0.2 fusion.19
  79.2 0.1 fusion.20
  79.4 1.4 %copy-done.7 = bf16[1024,1024]{1,0:T(8,128)(2,1)S(1)} copy-done((bf16[1024,1024]{1,0:T(8,128)(2,1)S(1)}, bf16[1024,1024]{1,0:T(8,128)(2,1)}, u32[]{:S(2)}) %copy-start.7) | copy-done | bytes 2097176
  80.8 2.6 %convolution_bitcast_fusion.1 = f32[1,512,1024]{2,1,0:T(8,128)} fusion(bf16[1024,1024]{1,0:T(8,128)(2,1)S(1)} %copy-done.7, bf16[1024,256]{1,0:T(8,128)(2,1)S(1)} %get-tuple-element.30, bf16[1024,256]{1,0:T(8,128)(2,1)S(1)} %get-tuple-element.27), kind=kOutput, calls=%fused_computation.5 | convolution fusion | flops 1075838976 | bytes 5242880 | tf_op jit(solution)/shard_map/sd,sf->df/dot_general | solution.py:311
  83.4 2.6 %convolution_bitcast_fusion = f32[1,1024,512]{2,1,0:T(8,128)} fusion(bf16[1024,1024]{1,0:T(8,128)(2,1)S(1)} %copy-done.9, bf16[1024,256]{1,0:T(8,128)(2,1)S(1)} %get-tuple-element.31, bf16[1024,256]{1,0:T(8,128)(2,1)S(1)} %get-tuple-element.26), kind=kOutput, calls=%fused_computation.4 | convolution fusion | flops 1075838976 | bytes 5242880 | tf_op jit(solution)/shard_map/sf,sd->fd/dot_general | solution.py:312
  86.0 0.2 collective-permute-done
  86.2 0.9 %pad_maximum_fusion = bf16[3,512,256]{2,1,0:T(8,128)(2,1)} fusion(bf16[3,256,256]{2,1,0:T(8,128)(2,1)S(1)} %collective-permute-done, bf16[3,256,256]{2,1,0:T(8,128)(2,1)S(1)} %get-tuple-element.20), kind=kLoop, calls=%fused_computation.17 | loop fusion | flops 1572864 | bytes 1572864 | tf_op jit(solution)/shard_map/concatenate | solution.py:371
  87.1 0.6 copy.13
  (12 shorter events, 0.0 us)
Async XLA Ops:
  0.6 2.0 %copy-start = (bf16[512,512]{1,0:T(8,128)(2,1)S(1)}, bf16[512,512]{1,0:T(8,128)(2,1)}, u32[]{:S(2)}) copy-start(bf16[512,512]{1,0:T(8,128)(2,1)} %param.8) | copy-start | bytes 1572868
  2.6 2.9 %copy-start.1 = (bf16[1,512,1024]{2,1,0:T(8,128)(2,1)S(1)}, bf16[1,512,1024]{2,1,0:T(8,128)(2,1)}, u32[]{:S(2)}) copy-start(bf16[1,512,1024]{2,1,0:T(8,128)(2,1)} %param.12) | copy-start | bytes 3145732
  2.6 2.9 %copy-start.5 = (f32[1,1024]{1,0:T(1,128)S(1)}, f32[1,1024]{1,0:T(1,128)}, u32[]{:S(2)}) copy-start(f32[1,1024]{1,0:T(1,128)} %b_ref.1) | copy-start | bytes 12292
  5.6 1.2 %copy-start.2 = (bf16[1,1024,512]{2,1,0:T(8,128)(2,1)S(1)}, bf16[1,1024,512]{2,1,0:T(8,128)(2,1)}, u32[]{:S(2)}) copy-start(bf16[1,1024,512]{2,1,0:T(8,128)(2,1)} %param.14) | copy-start | bytes 3145732
  6.8 1.1 %copy-start.3 = (bf16[3,512,256]{2,1,0:T(8,128)(2,1)S(1)}, bf16[3,512,256]{2,1,0:T(8,128)(2,1)}, u32[]{:S(2)}) copy-start(bf16[3,512,256]{2,1,0:T(8,128)(2,1)} %own_ref.1) | copy-start | bytes 2359300
  7.9 1.2 %copy-start.6 = (bf16[1024,512]{1,0:T(8,128)(2,1)S(1)}, bf16[1024,512]{1,0:T(8,128)(2,1)}, u32[]{:S(2)}) copy-start(bf16[1024,512]{1,0:T(8,128)(2,1)} %fusion.2) | copy-start | bytes 3145732
  9.1 59.1 %copy-start.4 = (bf16[3,512,256]{2,1,0:T(8,128)(2,1)S(1)}, bf16[3,512,256]{2,1,0:T(8,128)(2,1)}, u32[]{:S(2)}) copy-start(bf16[3,512,256]{2,1,0:T(8,128)(2,1)} %own_ref.1) | copy-start | bytes 2359300
  68.2 10.8 %copy-start.8 = (bf16[2,16,64,512]{3,2,1,0:T(8,128)(2,1)S(1)}, bf16[2,16,64,512]{3,2,1,0:T(8,128)(2,1)}, u32[]{:S(2)}) copy-start(bf16[2,16,64,512]{3,2,1,0:T(8,128)(2,1)} %get-tuple-element.13) | copy-start | bytes 6291460
  78.2 8.0 %collective-permute-start = (bf16[3,256,256]{2,1,0:T(8,128)(2,1)S(1)}, bf16[3,256,256]{2,1,0:T(8,128)(2,1)S(1)}, u32[]{:S(2)}, u32[]{:S(2)}) collective-permute-start(bf16[3,256,256]{2,1,0:T(8,128)(2,1)S(1)} %get-tuple-element.21), channel_id=1, source_target_pairs={{2,0},{4,2},{6,4},{8,6},{10,8},{12,10},{14,12},{16,14},{18,16},{20... | collective-permute-start | bytes 1179656 | tf_op jit(solution)/shard_map/ppermute | solution.py:20
  79.2 1.6 %copy-start.7 = (bf16[1024,1024]{1,0:T(8,128)(2,1)S(1)}, bf16[1024,1024]{1,0:T(8,128)(2,1)}, u32[]{:S(2)}) copy-start(bf16[1024,1024]{1,0:T(8,128)(2,1)} %get-tuple-element.14) | copy-start | bytes 6291460
  80.8 2.6 %copy-start.9 = (bf16[1024,1024]{1,0:T(8,128)(2,1)S(1)}, bf16[1024,1024]{1,0:T(8,128)(2,1)}, u32[]{:S(2)}) copy-start(bf16[1024,1024]{1,0:T(8,128)(2,1)} %get-tuple-element.16) | copy-start | bytes 6291460

commit v3 on v2

--- a/solution.py
+++ b/solution.py
@@ -40,26 +40,14 @@
     return (d_inputs, g_first, g_bias, g_second)
 
 
-def window_kernel(heads, bias_ref, edge_ref, own_ref, cot_edge_ref, cot_ref, back_ref, mine_ref,
-                  q_t, k_t, cot_t, dq_t, dk_sum, dv_sum):
-    lead = edge_ref.shape[1]
-    rows, cols = q_t.shape[1], q_t.shape[0]
+def window_probs(heads, lead, bias, keys, q_t, probs_ref):
+    cols, rows = q_t.shape
     head_dim = cols // heads
-    scale = head_dim ** (-0.5)
-    factor = scale * math.log2(math.e)
-    queries = jnp.concatenate([edge_ref[0], own_ref[0, : rows - lead]], axis=0)
-    keys = jnp.concatenate([edge_ref[1], own_ref[1, : rows - lead]], axis=0)
-    values = jnp.concatenate([edge_ref[2], own_ref[2, : rows - lead]], axis=0)
-    cot = jnp.concatenate([cot_edge_ref[...], cot_ref[: rows - lead]], axis=0)
-    q_t[...] = queries.T
-    k_t[...] = keys.T
-    cot_t[...] = cot.T
+    factor = head_dim ** (-0.5) * math.log2(math.e)
     column = lax.broadcasted_iota(jnp.int32, (1, cols), 1)
-    bias = bias_ref[0]
     for head in range(heads):
         own = (column // head_dim == head).astype(jnp.float32).astype(jnp.bfloat16)
-        keys_h, values_h, queries_h, cot_h = keys * own, values * own, queries * own, cot * own
-        d_k = d_v = None
+        keys_h = keys * own
         for part in range(2):
             span = slice(0, lead) if part == 0 else slice(lead, rows)
             scores = jnp.dot(keys_h, q_t[:, span], preferred_element_type=jnp.float32)
@@ -72,65 +60,115 @@
             peak = jnp.max(scores, axis=0, keepdims=True)
             expo = jnp.exp2((scores - peak) * factor)
             probs = expo * (1.0 / jnp.sum(expo, axis=0, keepdims=True))
+            probs_ref[head, :, span] = probs.astype(jnp.bfloat16)
+
+
+def probs_kernel(heads, bias_ref, edge_ref, own_ref, probs_ref, q_t):
+    lead, rows = edge_ref.shape[1], q_t.shape[1]
+    queries = jnp.concatenate([edge_ref[0], own_ref[0, : rows - lead]], axis=0)
+    keys = jnp.concatenate([edge_ref[1], own_ref[1, : rows - lead]], axis=0)
+    q_t[...] = queries.T
+    window_probs(heads, lead, bias_ref[0], keys, q_t, probs_ref)
+
+
+def separate_probs(bias, edge, own, heads):
+    _, rows, cols = own.shape
+    vmem = pl.BlockSpec(memory_space=pltpu.VMEM)
+    return pl.pallas_call(
+        functools.partial(probs_kernel, heads),
+        out_shape=jax.ShapeDtypeStruct((heads, rows, rows), jnp.bfloat16),
+        in_specs=[pl.BlockSpec(memory_space=pltpu.SMEM), vmem, vmem],
+        out_specs=vmem,
+        scratch_shapes=[pltpu.VMEM((cols, rows), jnp.bfloat16)],
+        compiler_params=pltpu.CompilerParams(vmem_limit_bytes=48 * 1024 * 1024),
+        name="window_probs",
+    )(bias, edge, own)
+
+
+def window_kernel(heads, probs_ref, edge_ref, own_ref, cot_edge_ref, cot_ref, back_ref, mine_ref,
+                  k_t, cot_t, dq_t):
+    lead = edge_ref.shape[1]
+    rows, cols = k_t.shape[1], k_t.shape[0]
+    head_dim = cols // heads
+    scale = head_dim ** (-0.5)
+    queries = jnp.concatenate([edge_ref[0], own_ref[0, : rows - lead]], axis=0)
+    keys = jnp.concatenate([edge_ref[1], own_ref[1, : rows - lead]], axis=0)
+    values = jnp.concatenate([edge_ref[2], own_ref[2, : rows - lead]], axis=0)
+    cot = jnp.concatenate([cot_edge_ref[...], cot_ref[: rows - lead]], axis=0)
+    k_t[...] = keys.T
+    cot_t[...] = cot.T
+    column = lax.broadcasted_iota(jnp.int32, (1, cols), 1)
+    d_k = d_v = None
+    for head in range(heads):
+        own = (column // head_dim == head).astype(jnp.float32).astype(jnp.bfloat16)
+        values_h, queries_h, cot_h = values * own, queries * own, cot * own
+        for part in range(2):
+            span = slice(0, lead) if part == 0 else slice(lead, rows)
+            probs_b = probs_ref[head, :, span]
+            probs = probs_b.astype(jnp.float32)
             d_probs = jnp.dot(values_h, cot_t[:, span], preferred_element_type=jnp.float32)
             delta = jnp.sum(probs * d_probs, axis=0, keepdims=True)
             d_scores = (probs * (d_probs - delta)).astype(jnp.bfloat16)
-            probs_b = probs.astype(jnp.bfloat16)
             mine = slice(head * head_dim, (head + 1) * head_dim)
             dq_t[mine, span] = jnp.dot(k_t[mine, :], d_scores, preferred_element_type=jnp.float32) * scale
             more_k = jnp.dot(d_scores, queries_h[span], preferred_element_type=jnp.float32)
             more_v = jnp.dot(probs_b, cot_h[span], preferred_element_type=jnp.float32)
             d_k = more_k if d_k is None else d_k + more_k
             d_v = more_v if d_v is None else d_v + more_v
-        if head == 0:
-            dk_sum[...] = d_k
-            dv_sum[...] = d_v
-        else:
-            dk_sum[...] += d_k
-            dv_sum[...] += d_v
     d_q = dq_t[...].T.astype(jnp.bfloat16)
-    d_k = (dk_sum[...] * scale).astype(jnp.bfloat16)
-    d_v = dv_sum[...].astype(jnp.bfloat16)
-    for place, grad in enumerate((d_q, d_k, d_v)):
+    for place, grad in enumerate((d_q, (d_k * scale).astype(jnp.bfloat16), d_v.astype(jnp.bfloat16))):
         back_ref[place] = grad[:lead]
         mine_ref[place] = grad[lead:]
 
 
-def window_grads(bias, edge, own, cot_edge, cot, heads):
+def window_grads(probs, edge, own, cot_edge, cot, part, parts):
     lead = edge.shape[1]
     rows, cols = cot.shape
+    heads, cols = probs.shape[0] // parts, cols // parts
     vmem = pl.BlockSpec(memory_space=pltpu.VMEM)
     return pl.pallas_call(
         functools.partial(window_kernel, heads),
+        grid=(1,),
         out_shape=(
             jax.ShapeDtypeStruct((3, lead, cols), jnp.bfloat16),
             jax.ShapeDtypeStruct((3, rows - lead, cols), jnp.bfloat16),
         ),
-        in_specs=[pl.BlockSpec(memory_space=pltpu.SMEM)] + [vmem] * 4,
+        in_specs=[
+            pl.BlockSpec((heads, rows, rows), lambda i: (part, 0, 0)),
+            pl.BlockSpec((3, lead, cols), lambda i: (0, 0, part)),
+            pl.BlockSpec((3, rows, cols), lambda i: (0, 0, part)),
+            pl.BlockSpec((lead, cols), lambda i: (0, part)),
+            pl.BlockSpec((rows, cols), lambda i: (0, part)),
+        ],
         out_specs=(vmem, vmem),
         scratch_shapes=[
             pltpu.VMEM((cols, rows), jnp.bfloat16),
             pltpu.VMEM((cols, rows), jnp.bfloat16),
-            pltpu.VMEM((cols, rows), jnp.bfloat16),
             pltpu.VMEM((cols, rows), jnp.float32),
-            pltpu.VMEM((rows, cols), jnp.float32),
-            pltpu.VMEM((rows, cols), jnp.float32),
         ],
         compiler_params=pltpu.CompilerParams(vmem_limit_bytes=48 * 1024 * 1024),
         cost_estimate=pl.CostEstimate(
-            flops=10 * rows * rows * cols, bytes_accessed=14 * rows * cols, transcendentals=heads * rows * rows
+            flops=8 * rows * rows * cols * heads, bytes_accessed=14 * rows * cols, transcendentals=0
         ),
         name="window_grads",
-    )(bias, edge, own, cot_edge, cot)
+    )(probs, edge, own, cot_edge, cot)
+
 
 MESH = pl.DeviceIdType.MESH
 
 
-def exchange_kernel(n, group, send_ref, qkv_ref, w_in_ref, b_ref, w_out_ref, place_t_ref, grad_ref,
-                    got_ref, dact_ref, hidden_ref, gb_ref, edge_ref, cot_edge_ref, heads_ref,
+def exchange_kernel(n, group, heads, qkv_hbm, w_in_hbm, w_out_hbm, x_ref, grad_ref, gate_ref, route_ref, b_ref,
+                    got_ref, dact_ref, hidden_ref, gb_ref, edge_ref, cot_edge_ref, heads_ref, probs_ref,
+                    send_ref, place_t_ref, qkv_ref, w_in_ref, w_out_ref, q_t,
                     w_in_t, w_out_t, part_out, part_in, ret_out, ret_in,
                     send_sem, recv_sem, on_send, on_recv, part_send, part_recv, ret_send, ret_recv,
-                    edge_sem, cot_sem, own_sem):
+                    edge_sem, cot_sem, own_sem, load_sem):
+    loads = [
+        pltpu.make_async_copy(src, dst, load_sem.at[i])
+        for i, (src, dst) in enumerate(((qkv_hbm, qkv_ref), (w_in_hbm, w_in_ref), (w_out_hbm, w_out_ref)))
+    ]
+    for load in loads:
+        load.start()
     me, core = lax.axis_index("ex"), lax.axis_index("hh")
     after, sibling = lax.rem(me + 1, n), 1 - core
     capacity, half = ret_in.shape[1], ret_in.shape[2]
@@ -153,6 +191,29 @@
         pl.semaphore_signal(barrier, inc=1, device_id=(partners[k], core), device_id_type=MESH)
     pl.semaphore_signal(barrier, inc=1, device_id=(me, sibling), device_id_type=MESH)
     pl.semaphore_wait(barrier, n)
+    edge = pltpu.make_async_remote_copy(
+        src_ref=qkv_hbm.at[:, pl.ds(start, lead)], dst_ref=edge_ref, send_sem=edge_sem.at[0],
+        recv_sem=edge_sem.at[1], device_id=(after, core), device_id_type=MESH,
+    )
+    edge.start()
+
+    tokens, width = x_ref.shape
+    route = route_ref[...].astype(jnp.float32)
+    expert = lax.broadcasted_iota(jnp.int32, (1, 128), 1).astype(jnp.float32)
+    onehot = (route == expert).astype(jnp.float32)
+    earlier = (
+        lax.broadcasted_iota(jnp.int32, (tokens, tokens), 0) > lax.broadcasted_iota(jnp.int32, (tokens, tokens), 1)
+    ).astype(jnp.float32).astype(jnp.bfloat16)
+    before = jnp.dot(earlier, onehot.astype(jnp.bfloat16), preferred_element_type=jnp.float32)
+    dest = route * float(capacity) + jnp.sum(before * onehot, axis=1, keepdims=True)
+    slot = lax.broadcasted_iota(jnp.int32, (1, n * capacity), 1).astype(jnp.float32)
+    place_t = (dest == slot).astype(jnp.float32).astype(jnp.bfloat16)
+    place_t_ref[...] = place_t
+    own_x = jnp.where(core == 0, x_ref[:, :half], x_ref[:, half:])
+    own_grad = jnp.where(core == 0, grad_ref[:, :half], grad_ref[:, half:]).astype(jnp.float32)
+    own_s = (gate_ref[...] * own_grad).astype(jnp.bfloat16)
+    ready = jnp.dot(place_t.T, jnp.concatenate([own_x, own_s], axis=1), preferred_element_type=jnp.float32)
+    send_ref[...] = ready.astype(jnp.bfloat16).reshape(n, capacity, 2 * half)
 
     def remote(src, dst, send, recv, device):
         return pltpu.make_async_remote_copy(
@@ -173,14 +234,14 @@
     near = list(range(1, n // 2))
     order = []
     while far or near:
-        order += far[:2] + near[:1]
-        far, near = far[2:], near[1:]
+        order += near[:1] + far[:1]
+        far, near = far[1:], near[1:]
     for k in order:
         out[k].start()
     own = pltpu.make_async_copy(send_ref.at[me], got_ref.at[core, me], own_sem.at[0])
     own.start()
-    edge = remote(qkv_ref.at[:, pl.ds(start, lead)], edge_ref, edge_sem.at[0], edge_sem.at[1], (after, core))
-    edge.start()
+    for load in loads:
+        load.wait()
     w_in_t[...] = w_in_ref[...].T
     w_out_t[...] = w_out_ref[...].T
 
@@ -232,10 +293,18 @@
                 back[k] = remote(ret_out.at[partners[k]], ret_in.at[me], ret_send.at[k], ret_recv.at[k],
                                  (partners[k], core))
             back[k].start()
+        if g == 1:
+            edge.wait_recv()
+            window = qkv_ref.shape[1]
+            queries = jnp.concatenate([edge_ref[0], qkv_ref[0, : window - lead]], axis=0)
+            keys = jnp.concatenate([edge_ref[1], qkv_ref[1, : window - lead]], axis=0)
+            q_t[...] = queries.T
+            bias = jnp.where(me == 0, -1e30, 0.0).astype(jnp.float32)
+            window_probs(heads, lead, bias, keys, q_t, probs_ref)
     for c in range(4):
         gb_ref[:, c * step : (c + 1) * step] = bias_sums[c]
 
-    total = grad_ref[...].astype(jnp.float32)
+    total = jnp.where(core == 0, grad_ref[:, :half], grad_ref[:, half:]).astype(jnp.float32)
     for g in range(n // group):
         for k in range(g * group, (g + 1) * group):
             if k == 0:
@@ -258,21 +327,22 @@
             back[k].wait_send()
     for swap in parts:
         swap.wait_send()
-    edge.wait()
+    edge.wait_send()
     cot.wait()
 
 
-def exchange(send, qkv, w_in, b_in, w_out, place_t, own_grad, lead):
-    n, capacity, columns = send.shape
-    half = columns // 2
-    width, hidden_units = w_in.shape
+def exchange(qkv, w_in, w_out, x, grad, gate, route, b_in, n, capacity, lead, heads):
+    tokens, width = x.shape
+    hidden_units = w_in.shape[1]
+    half = qkv.shape[2]
+    columns = 2 * half
     group = 4
     vmem = pl.BlockSpec(memory_space=pltpu.VMEM)
     bf16, f32 = jnp.bfloat16, jnp.float32
     dma = pltpu.SemaphoreType.DMA
     shape = jax.ShapeDtypeStruct
     return pl.pallas_call(
-        functools.partial(exchange_kernel, n, group),
+        functools.partial(exchange_kernel, n, group, heads),
         out_shape=(
             shape((2, n, capacity, columns), bf16),
             shape((n * capacity, hidden_units), bf16),
@@ -280,11 +350,18 @@
             shape((1, hidden_units), f32),
             shape((3, lead, half), bf16),
             shape((lead, half), bf16),
-            shape(own_grad.shape, bf16),
+            shape((tokens, half), bf16),
+            shape((heads, tokens, tokens), bf16),
         ),
-        in_specs=[vmem] * 7,
-        out_specs=[vmem] * 7,
+        in_specs=[pl.BlockSpec(memory_space=pl.ANY)] * 3 + [vmem] * 5,
+        out_specs=[vmem] * 8,
         scratch_shapes=[
+            pltpu.VMEM((n, capacity, columns), bf16),
+            pltpu.VMEM((tokens, n * capacity), bf16),
+            pltpu.VMEM(qkv.shape, bf16),
+            pltpu.VMEM(w_in.shape, bf16),
+            pltpu.VMEM(w_out.shape, bf16),
+            pltpu.VMEM((half, tokens), bf16),
             pltpu.VMEM((hidden_units, width), bf16),
             pltpu.VMEM((width, hidden_units), bf16),
             pltpu.VMEM((n // group, group * capacity, half), bf16),
@@ -294,7 +371,7 @@
             dma((n,)), dma((n,)), dma((n,)), dma((n,)),
             dma((n // group,)), dma((n // group,)),
             dma((n,)), dma((n,)),
-            dma((2,)), dma((2,)), dma((2,)),
+            dma((2,)), dma((2,)), dma((2,)), dma((3,)),
         ],
         compiler_params=pltpu.CompilerParams(
             collective_id=0, has_side_effects=True, vmem_limit_bytes=48 * 1024 * 1024
@@ -304,7 +381,7 @@
             transcendentals=2 * n * capacity * hidden_units,
         ),
         name="exchange",
-    )(send, qkv, w_in, b_in, w_out, place_t, own_grad)
+    )(qkv, w_in, w_out, x, grad, gate, route, b_in)
 
 
 def weight_grads(x, s, d_act, hidden):
@@ -328,28 +405,28 @@
     heads_here = HEADS // lax.axis_size("hh")
     lead = SHIFT * CELLS
     start = WIN_T * CELLS - lead
-    choose = route[:, 0]
-    onehot = (choose[:, None] == jnp.arange(experts, dtype=jnp.int32)[None, :]).astype(jnp.bfloat16)
-    earlier = (jnp.arange(tok_rows)[:, None] > jnp.arange(tok_rows)[None, :]).astype(jnp.bfloat16)
-    before = jnp.dot(earlier, onehot, preferred_element_type=jnp.float32)
-    slots = jnp.sum(before * onehot.astype(jnp.float32), axis=1).astype(jnp.int32)
-    dest = choose * capacity + slots
-    place = (dest[None, :] == jnp.arange(experts * capacity, dtype=jnp.int32)[:, None]).astype(jnp.bfloat16)
-    own_x = lax.dynamic_slice_in_dim(moe_input, member * half, half, 1)
-    own_grad = lax.dynamic_slice_in_dim(out_grad, member * half, half, 1)
-    own_s = (gate[:, None] * own_grad.astype(jnp.float32)).astype(jnp.bfloat16)
-    tokens = jnp.concatenate([own_x, own_s], axis=1)
-    send = jnp.dot(place, tokens, preferred_element_type=jnp.float32).astype(jnp.bfloat16)
-    send = send.reshape(experts, capacity, 2 * half)
     if capacity % 16 == 0 and experts % 4 == 0 and experts & (experts - 1) == 0:
-        got, d_act, hidden, g_bias, qkv_edge, cot_edge, d_heads = exchange(
-            send, qkv, w_in[0], b_in, w_out[0], place.T, own_grad, lead
+        got, d_act, hidden, g_bias, qkv_edge, cot_edge, d_heads, probs = exchange(
+            qkv, w_in[0], w_out[0], moe_input, out_grad, gate[:, None], route, b_in, experts, capacity, lead, heads_here
         )
         g_bias = g_bias[0]
         got = got.reshape(2, experts * capacity, 2 * half)
         got_x, got_s = columns_joined(got[0], got[1], half)
         g_first, g_second = weight_grads(got_x, got_s, d_act, hidden)
     else:
+        choose = route[:, 0]
+        onehot = (choose[:, None] == jnp.arange(experts, dtype=jnp.int32)[None, :]).astype(jnp.bfloat16)
+        earlier = (jnp.arange(tok_rows)[:, None] > jnp.arange(tok_rows)[None, :]).astype(jnp.bfloat16)
+        before = jnp.dot(earlier, onehot, preferred_element_type=jnp.float32)
+        slots = jnp.sum(before * onehot.astype(jnp.float32), axis=1).astype(jnp.int32)
+        dest = choose * capacity + slots
+        place = (dest[None, :] == jnp.arange(experts * capacity, dtype=jnp.int32)[:, None]).astype(jnp.bfloat16)
+        own_x = lax.dynamic_slice_in_dim(moe_input, member * half, half, 1)
+        own_grad = lax.dynamic_slice_in_dim(out_grad, member * half, half, 1)
+        own_s = (gate[:, None] * own_grad.astype(jnp.float32)).astype(jnp.bfloat16)
+        tokens = jnp.concatenate([own_x, own_s], axis=1)
+        send = jnp.dot(place, tokens, preferred_element_type=jnp.float32).astype(jnp.bfloat16)
+        send = send.reshape(experts, capacity, 2 * half)
         qkv_edge = passed_along(qkv[:, start:], "ex", 1)
         got = lax.all_to_all(send, "ex", split_axis=0, concat_axis=0, tiled=True)
         got = got.reshape(experts * capacity, 2 * half)
@@ -366,9 +443,13 @@
         d_moe = lax.dot_general(place, returned, (((0,), (0,)), ((), ())), preferred_element_type=jnp.float32)
         d_heads = (own_grad.astype(jnp.float32) + d_moe).astype(jnp.bfloat16)
         cot_edge = passed_along(d_heads[start:], "ex", 1)
-    bias = jnp.where(lax.axis_index("ex") == 0, -1e30, 0.0).astype(jnp.float32).reshape(1)
-    back, mine = window_grads(bias, qkv_edge, qkv, cot_edge, d_heads, heads_here)
-    g_qkv = jnp.concatenate([mine, passed_along(back, "ex", -1)], axis=1)
+        bias = jnp.where(lax.axis_index("ex") == 0, -1e30, 0.0).astype(jnp.float32).reshape(1)
+        probs = separate_probs(bias, qkv_edge, qkv, heads_here)
+    pieces = []
+    for part in range(2):
+        back, mine = window_grads(probs, qkv_edge, qkv, cot_edge, d_heads, part, 2)
+        pieces.append(jnp.concatenate([mine, passed_along(back, "ex", -1)], axis=1))
+    g_qkv = jnp.concatenate(pieces, axis=2)
     return (g_first[None], g_bias[None], g_second[None], g_qkv)
 
 

time: 88.1 us -> 96.9 us (1.100)
  local copies, waits for them, and re-layouts: 5.97 us -> 12.5 us
  Pallas kernels: 69.1 us -> 73.2 us
  starting transfers between devices: 0.81 us -> 3.85 us
  matrix products: 7.9 us -> 5.19 us
  other arithmetic: 3.04 us -> 0.98 us
    unnamed x21 -> x22, local copies, waits for them, and re-layouts: 5.65 us -> 11.4 us
    pallas_call x2 -> x3, Pallas kernels: 69.1 us -> 73.2 us  [the longest x1 64 us: exchange(): pl.pallas_call(functools.partial(exchange_kernel, n, group, heads), out_s...]
    ppermute x1 -> x2, starting transfers between devices: 0.81 us -> 3.85 us  [passed_along(): return lax.ppermute(block, axis, route)]
    dot_general x2 -> x0, matrix products: 2.71 us -> none  [the longest x1 1.68 us: local(): jnp.dot(place, tokens, preferred_element_type=jnp.float32)]
    convert_element_type x2 -> x0, other arithmetic: 1.42 us -> none  [the longest x1 1.18 us: local(): own_s = (gate[:, None] * own_grad.astype(jnp.float32)).astype(jnp.bfloat16)]
  transfers between devices with their start and end apart: 1 -> 2, of which waited for: 1 -> 0; matrix products, arithmetic and copies ran while one was open for 6% -> 6% of each run, Pallas kernels for 0% -> 5%
where the time goes in v3:
time: 96.9 us; the launch traced here: 96.4 us
  Pallas kernels  73.2 us (76%)
  local copies, waits for them, and re-layouts  12.5 us (13%)
  matrix products  5.19 us (5%)
  starting transfers between devices  3.85 us (4%)
  other arithmetic  0.98 us (1%)
    pallas_call x1, Pallas kernels, exchange(): pl.pallas_call(functools.partial(exchange_kernel, n, group, heads), out_s...  64 us
    unnamed x22, local copies, waits for them, and re-layouts  11.4 us
    pallas_call x2, Pallas kernels, window_grads(): pl.pallas_call(functools.partial(window_kernel, heads), grid=(1,), out_sh...  9.19 us
    ppermute x2, starting transfers between devices, passed_along(): return lax.ppermute(block, axis, route)  3.85 us
    dot_general x1, matrix products, weight_grads(): jnp.einsum('sf,sd->fd', hidden, s, preferred_element_type=jnp.float32)  2.61 us
    dot_general x1, matrix products, weight_grads(): jnp.einsum('sd,sf->df', x, d_act, preferred_element_type=jnp.float32)  2.59 us
  transfers between devices with their start and end apart: 2, of which 0 were waited for; matrix products, arithmetic and copies ran while one was open for 6% of the time, Pallas kernels for 5%

profile of v3, /device:TPU:0, one launch (start us, length us, event | category | flops | bytes accessed | tf_op | source)
XLA Modules:
  0.0 96.4 jit_solution(2293384675516936920)
XLA Ops:
  0.6 0.8 copy.13.gate_ref
  1.5 0.8 copy.14.route_ref
  2.3 0.0 copy-start.1
  2.3 1.1 %copy-done.1 = bf16[3,512,256]{2,1,0:T(8,128)(2,1)S(1)} copy-done((bf16[3,512,256]{2,1,0:T(8,128)(2,1)S(1)}, bf16[3,512,256]{2,1,0:T(8,128)(2,1)}, u32[]{:S(2)}) %copy-start.1) | copy-done | bytes 786456
  3.4 1.2 %copy-done.2 = bf16[1,512,1024]{2,1,0:T(8,128)(2,1)S(1)} copy-done((bf16[1,512,1024]{2,1,0:T(8,128)(2,1)S(1)}, bf16[1,512,1024]{2,1,0:T(8,128)(2,1)}, u32[]{:S(2)}) %copy-start.2) | copy-done | bytes 1048600
  4.7 1.2 %copy-done.3 = bf16[1,1024,512]{2,1,0:T(8,128)(2,1)S(1)} copy-done((bf16[1,1024,512]{2,1,0:T(8,128)(2,1)S(1)}, bf16[1,1024,512]{2,1,0:T(8,128)(2,1)}, u32[]{:S(2)}) %copy-start.3) | copy-done | bytes 1048600
  5.9 1.0 %copy-done.4 = bf16[512,512]{1,0:T(8,128)(2,1)S(1)} copy-done((bf16[512,512]{1,0:T(8,128)(2,1)S(1)}, bf16[512,512]{1,0:T(8,128)(2,1)}, u32[]{:S(2)}) %copy-start.4) | copy-done | bytes 524312
  6.9 1.0 %copy-done.5 = bf16[512,512]{1,0:T(8,128)(2,1)S(1)} copy-done((bf16[512,512]{1,0:T(8,128)(2,1)S(1)}, bf16[512,512]{1,0:T(8,128)(2,1)}, u32[]{:S(2)}) %copy-start.5) | copy-done | bytes 524312
  8.0 0.7 copy-done.6
  8.7 64.0 %exchange.1 = (bf16[2,16,64,512]{3,2,1,0:T(8,128)(2,1)}, bf16[1024,1024]{1,0:T(8,128)(2,1)}, bf16[1024,1024]{1,0:T(8,128)(2,1)}, f32[1,1024]{1,0:T(1,128)S(1)}, ...) custom-call(bf16[3,512,256]{2,1,0:T(8,128)(2,1)S(1)} %copy-done.1, ...), custom_call_target="tpu_custom_call" | custom-call | flops 3221225472 | bytes 16777216 | tf_op jit(solution)/shard_map/exchange/pallas_call | solution.py:344
  72.7 2.2 %copy-done = bf16[8,512,512]{2,1,0:T(8,128)(2,1)S(1)} copy-done((bf16[8,512,512]{2,1,0:T(8,128)(2,1)S(1)}, bf16[8,512,512]{2,1,0:T(8,128)(2,1)}, u32[]{:S(2)}) %copy-start) | copy-done | bytes 4194328
  74.8 4.6 %window_grads.2 = (bf16[3,256,128]{2,1,0:T(8,128)(2,1)S(1)}, bf16[3,256,128]{2,1,0:T(8,128)(2,1)S(1)}) custom-call(bf16[8,512,512]{2,1,0:T(8,128)(2,1)S(1)} %copy-done, bf16[3,256,256]{2,1,0:T(8,128)(2,1)S(1)} %get-tuple-element.21.edge_ref, bf16[3,512,256]{2,1,0:T(8,128)(2,1)S(1)} %copy-done.1, bf16[256,256]{1,0:T(8,128)(2,1)S(1)} %get-tuple-element.22.cot_edge_ref, ...), custom_call_target="tpu_custom_call" | custom-call | flops 1073741824 | bytes 917504 | tf_op jit(solution)/shard_map/window_grads/pallas_call | solution.py:129
  79.5 1.3 %collective-permute-start = (bf16[3,256,128]{2,1,0:T(8,128)(2,1)S(1)}, bf16[3,256,128]{2,1,0:T(8,128)(2,1)S(1)}, u32[]{:S(2)}, u32[]{:S(2)}) collective-permute-start(bf16[3,256,128]{2,1,0:T(8,128)(2,1)S(1)} %get-tuple-element.25), channel_id=1, source_target_pairs={{2,0},{4,2},{6,4},{8,6},{10,8},{12,10},{14,12},{16,14},{18,16},{20... | collective-permute-start | bytes 589832 | tf_op jit(solution)/shard_map/ppermute | solution.py:20
  80.7 4.6 %window_grads.3 = (bf16[3,256,128]{2,1,0:T(8,128)(2,1)S(1)}, bf16[3,256,128]{2,1,0:T(8,128)(2,1)S(1)}) custom-call(bf16[8,512,512]{2,1,0:T(8,128)(2,1)S(1)} %copy-done, bf16[3,256,256]{2,1,0:T(8,128)(2,1)S(1)} %get-tuple-element.21.edge_ref, bf16[3,512,256]{2,1,0:T(8,128)(2,1)S(1)} %copy-done.1, bf16[256,256]{1,0:T(8,128)(2,1)S(1)} %get-tuple-element.22.cot_edge_ref, ...), custom_call_target="tpu_custom_call" | custom-call | flops 1073741824 | bytes 917504 | tf_op jit(solution)/shard_map/window_grads/pallas_call | solution.py:129
  85.3 2.6 %collective-permute-start.1 = (bf16[3,256,128]{2,1,0:T(8,128)(2,1)S(1)}, bf16[3,256,128]{2,1,0:T(8,128)(2,1)S(1)}, u32[]{:S(2)}, u32[]{:S(2)}) collective-permute-start(bf16[3,256,128]{2,1,0:T(8,128)(2,1)S(1)} %get-tuple-element.27), channel_id=1, source_target_pairs={{2,0},{4,2},{6,4},{8,6},{10,8},{12,10},{14,12},{16,14},{18,16},{20... | collective-permute-start | bytes 589832 | tf_op jit(solution)/shard_map/ppermute | solution.py:20
  87.9 0.1 fusion.8
  88.1 0.1 fusion.9
  88.2 1.4 %copy-done.9 = bf16[1024,1024]{1,0:T(8,128)(2,1)S(1)} copy-done((bf16[1024,1024]{1,0:T(8,128)(2,1)S(1)}, bf16[1024,1024]{1,0:T(8,128)(2,1)}, u32[]{:S(2)}) %copy-start.9) | copy-done | bytes 2097176
  89.6 2.6 %convolution_bitcast_fusion = f32[1,1024,512]{2,1,0:T(8,128)} fusion(bf16[1024,1024]{1,0:T(8,128)(2,1)S(1)} %copy-done.9, bf16[1024,256]{1,0:T(8,128)(2,1)S(1)} %get-tuple-element.35, bf16[1024,256]{1,0:T(8,128)(2,1)S(1)} %get-tuple-element.30), kind=kOutput, calls=%fused_computation | convolution fusion | flops 1075838976 | bytes 5242880 | tf_op jit(solution)/shard_map/sf,sd->fd/dot_general | solution.py:389
  92.2 2.6 %convolution_bitcast_fusion.1 = f32[1,512,1024]{2,1,0:T(8,128)} fusion(bf16[1024,1024]{1,0:T(8,128)(2,1)S(1)} %copy-done.7, bf16[1024,256]{1,0:T(8,128)(2,1)S(1)} %get-tuple-element.34, bf16[1024,256]{1,0:T(8,128)(2,1)S(1)} %get-tuple-element.31), kind=kOutput, calls=%fused_computation.1 | convolution fusion | flops 1075838976 | bytes 5242880 | tf_op jit(solution)/shard_map/sd,sf->df/dot_general | solution.py:388
  94.8 0.0 collective-permute-done
  94.8 0.0 collective-permute-done.1
  94.8 1.0 %maximum_maximum_fusion = bf16[3,512,256]{2,1,0:T(8,128)(2,1)} fusion(bf16[3,256,128]{2,1,0:T(8,128)(2,1)S(1)} %collective-permute-done.1, bf16[3,256,128]{2,1,0:T(8,128)(2,1)S(1)} %get-tuple-element.26, bf16[3,256,128]{2,1,0:T(8,128)(2,1)S(1)} %collective-permute-done, bf16[3,256,128]{2,1,0:T(8,128)(2,1)S(1)} %get-tuple-element.24), kind=kLoop, calls=%fused_computation.8 | loop fusion | flops 3145728 | bytes 1572864 | tf_op jit(solution)/shard_map/concatenate | solution.py:452
  95.8 0.6 copy.16
  (11 shorter events, 0.0 us)
Async XLA Ops:
  2.3 1.1 %copy-start.1 = (bf16[3,512,256]{2,1,0:T(8,128)(2,1)S(1)}, bf16[3,512,256]{2,1,0:T(8,128)(2,1)}, u32[]{:S(2)}) copy-start(bf16[3,512,256]{2,1,0:T(8,128)(2,1)} %own_ref.3) | copy-start | bytes 2359300
  3.4 1.2 %copy-start.2 = (bf16[1,512,1024]{2,1,0:T(8,128)(2,1)S(1)}, bf16[1,512,1024]{2,1,0:T(8,128)(2,1)}, u32[]{:S(2)}) copy-start(bf16[1,512,1024]{2,1,0:T(8,128)(2,1)} %param.12) | copy-start | bytes 3145732
  4.7 1.2 %copy-start.3 = (bf16[1,1024,512]{2,1,0:T(8,128)(2,1)S(1)}, bf16[1,1024,512]{2,1,0:T(8,128)(2,1)}, u32[]{:S(2)}) copy-start(bf16[1,1024,512]{2,1,0:T(8,128)(2,1)} %param.14) | copy-start | bytes 3145732
  5.9 1.0 %copy-start.4 = (bf16[512,512]{1,0:T(8,128)(2,1)S(1)}, bf16[512,512]{1,0:T(8,128)(2,1)}, u32[]{:S(2)}) copy-start(bf16[512,512]{1,0:T(8,128)(2,1)} %x_ref.1) | copy-start | bytes 1572868
  6.9 1.0 %copy-start.5 = (bf16[512,512]{1,0:T(8,128)(2,1)S(1)}, bf16[512,512]{1,0:T(8,128)(2,1)}, u32[]{:S(2)}) copy-start(bf16[512,512]{1,0:T(8,128)(2,1)} %grad_ref.1) | copy-start | bytes 1572868
  8.0 0.7 copy-start.6
  72.7 2.2 %copy-start = (bf16[8,512,512]{2,1,0:T(8,128)(2,1)S(1)}, bf16[8,512,512]{2,1,0:T(8,128)(2,1)}, u32[]{:S(2)}) copy-start(bf16[8,512,512]{2,1,0:T(8,128)(2,1)} %get-tuple-element.20.probs_ref) | copy-start | bytes 12582916
  79.4 8.5 %copy-start.8 = (bf16[2,16,64,512]{3,2,1,0:T(8,128)(2,1)S(1)}, bf16[2,16,64,512]{3,2,1,0:T(8,128)(2,1)}, u32[]{:S(2)}) copy-start(bf16[2,16,64,512]{3,2,1,0:T(8,128)(2,1)} %get-tuple-element.16) | copy-start | bytes 6291460
  79.5 15.4 %collective-permute-start = (bf16[3,256,128]{2,1,0:T(8,128)(2,1)S(1)}, bf16[3,256,128]{2,1,0:T(8,128)(2,1)S(1)}, u32[]{:S(2)}, u32[]{:S(2)}) collective-permute-start(bf16[3,256,128]{2,1,0:T(8,128)(2,1)S(1)} %get-tuple-element.25), channel_id=1, source_target_pairs={{2,0},{4,2},{6,4},{8,6},{10,8},{12,10},{14,12},{16,14},{18,16},{20... | collective-permute-start | bytes 589832 | tf_op jit(solution)/shard_map/ppermute | solution.py:20
  85.3 9.5 %collective-permute-start.1 = (bf16[3,256,128]{2,1,0:T(8,128)(2,1)S(1)}, bf16[3,256,128]{2,1,0:T(8,128)(2,1)S(1)}, u32[]{:S(2)}, u32[]{:S(2)}) collective-permute-start(bf16[3,256,128]{2,1,0:T(8,128)(2,1)S(1)} %get-tuple-element.27), channel_id=1, source_target_pairs={{2,0},{4,2},{6,4},{8,6},{10,8},{12,10},{14,12},{16,14},{18,16},{20... | collective-permute-start | bytes 589832 | tf_op jit(solution)/shard_map/ppermute | solution.py:20
  88.0 1.6 %copy-start.9 = (bf16[1024,1024]{1,0:T(8,128)(2,1)S(1)}, bf16[1024,1024]{1,0:T(8,128)(2,1)}, u32[]{:S(2)}) copy-start(bf16[1024,1024]{1,0:T(8,128)(2,1)} %get-tuple-element.19) | copy-start | bytes 6291460
  89.6 2.6 %copy-start.7 = (bf16[1024,1024]{1,0:T(8,128)(2,1)S(1)}, bf16[1024,1024]{1,0:T(8,128)(2,1)}, u32[]{:S(2)}) copy-start(bf16[1024,1024]{1,0:T(8,128)(2,1)} %get-tuple-element.17) | copy-start | bytes 6291460

commit v4 on v3

--- a/solution.py
+++ b/solution.py
@@ -40,72 +40,38 @@
     return (d_inputs, g_first, g_bias, g_second)
 
 
-def window_probs(heads, lead, bias, keys, q_t, probs_ref):
-    cols, rows = q_t.shape
-    head_dim = cols // heads
-    factor = head_dim ** (-0.5) * math.log2(math.e)
-    column = lax.broadcasted_iota(jnp.int32, (1, cols), 1)
-    for head in range(heads):
-        own = (column // head_dim == head).astype(jnp.float32).astype(jnp.bfloat16)
-        keys_h = keys * own
-        for part in range(2):
-            span = slice(0, lead) if part == 0 else slice(lead, rows)
-            scores = jnp.dot(keys_h, q_t[:, span], preferred_element_type=jnp.float32)
-            low, high = scores[:lead], scores[lead:]
-            if part == 0:
-                high = high + bias
-            else:
-                low = low + bias
-            scores = jnp.concatenate([low, high], axis=0)
-            peak = jnp.max(scores, axis=0, keepdims=True)
-            expo = jnp.exp2((scores - peak) * factor)
-            probs = expo * (1.0 / jnp.sum(expo, axis=0, keepdims=True))
-            probs_ref[head, :, span] = probs.astype(jnp.bfloat16)
-
-
-def probs_kernel(heads, bias_ref, edge_ref, own_ref, probs_ref, q_t):
-    lead, rows = edge_ref.shape[1], q_t.shape[1]
-    queries = jnp.concatenate([edge_ref[0], own_ref[0, : rows - lead]], axis=0)
-    keys = jnp.concatenate([edge_ref[1], own_ref[1, : rows - lead]], axis=0)
-    q_t[...] = queries.T
-    window_probs(heads, lead, bias_ref[0], keys, q_t, probs_ref)
-
-
-def separate_probs(bias, edge, own, heads):
-    _, rows, cols = own.shape
-    vmem = pl.BlockSpec(memory_space=pltpu.VMEM)
-    return pl.pallas_call(
-        functools.partial(probs_kernel, heads),
-        out_shape=jax.ShapeDtypeStruct((heads, rows, rows), jnp.bfloat16),
-        in_specs=[pl.BlockSpec(memory_space=pltpu.SMEM), vmem, vmem],
-        out_specs=vmem,
-        scratch_shapes=[pltpu.VMEM((cols, rows), jnp.bfloat16)],
-        compiler_params=pltpu.CompilerParams(vmem_limit_bytes=48 * 1024 * 1024),
-        name="window_probs",
-    )(bias, edge, own)
-
-
-def window_kernel(heads, probs_ref, edge_ref, own_ref, cot_edge_ref, cot_ref, back_ref, mine_ref,
-                  k_t, cot_t, dq_t):
+def window_kernel(heads, bias_ref, edge_ref, own_ref, cot_edge_ref, cot_ref, back_ref, mine_ref,
+                  q_t, k_t, cot_t, dq_t):
     lead = edge_ref.shape[1]
     rows, cols = k_t.shape[1], k_t.shape[0]
     head_dim = cols // heads
     scale = head_dim ** (-0.5)
+    factor = scale * math.log2(math.e)
     queries = jnp.concatenate([edge_ref[0], own_ref[0, : rows - lead]], axis=0)
     keys = jnp.concatenate([edge_ref[1], own_ref[1, : rows - lead]], axis=0)
     values = jnp.concatenate([edge_ref[2], own_ref[2, : rows - lead]], axis=0)
     cot = jnp.concatenate([cot_edge_ref[...], cot_ref[: rows - lead]], axis=0)
+    q_t[...] = queries.T
     k_t[...] = keys.T
     cot_t[...] = cot.T
     column = lax.broadcasted_iota(jnp.int32, (1, cols), 1)
     d_k = d_v = None
     for head in range(heads):
         own = (column // head_dim == head).astype(jnp.float32).astype(jnp.bfloat16)
-        values_h, queries_h, cot_h = values * own, queries * own, cot * own
+        keys_h, values_h, queries_h, cot_h = keys * own, values * own, queries * own, cot * own
         for part in range(2):
             span = slice(0, lead) if part == 0 else slice(lead, rows)
-            probs_b = probs_ref[head, :, span]
-            probs = probs_b.astype(jnp.float32)
+            scores = jnp.dot(keys_h, q_t[:, span], preferred_element_type=jnp.float32)
+            low, high = scores[:lead], scores[lead:]
+            if part == 0:
+                high = high + bias_ref[0]
+            else:
+                low = low + bias_ref[0]
+            scores = jnp.concatenate([low, high], axis=0)
+            peak = jnp.max(scores, axis=0, keepdims=True)
+            expo = jnp.exp2((scores - peak) * factor)
+            probs = expo * (1.0 / jnp.sum(expo, axis=0, keepdims=True))
+            probs_b = probs.astype(jnp.bfloat16)
             d_probs = jnp.dot(values_h, cot_t[:, span], preferred_element_type=jnp.float32)
             delta = jnp.sum(probs * d_probs, axis=0, keepdims=True)
             d_scores = (probs * (d_probs - delta)).astype(jnp.bfloat16)
@@ -121,10 +87,10 @@
         mine_ref[place] = grad[lead:]
 
 
-def window_grads(probs, edge, own, cot_edge, cot, part, parts):
+def window_grads(bias, edge, own, cot_edge, cot, heads, part, parts):
     lead = edge.shape[1]
     rows, cols = cot.shape
-    heads, cols = probs.shape[0] // parts, cols // parts
+    heads, cols = heads // parts, cols // parts
     vmem = pl.BlockSpec(memory_space=pltpu.VMEM)
     return pl.pallas_call(
         functools.partial(window_kernel, heads),
@@ -134,7 +100,7 @@
             jax.ShapeDtypeStruct((3, rows - lead, cols), jnp.bfloat16),
         ),
         in_specs=[
-            pl.BlockSpec((heads, rows, rows), lambda i: (part, 0, 0)),
+            pl.BlockSpec(memory_space=pltpu.SMEM),
             pl.BlockSpec((3, lead, cols), lambda i: (0, 0, part)),
             pl.BlockSpec((3, rows, cols), lambda i: (0, 0, part)),
             pl.BlockSpec((lead, cols), lambda i: (0, part)),
@@ -144,28 +110,30 @@
         scratch_shapes=[
             pltpu.VMEM((cols, rows), jnp.bfloat16),
             pltpu.VMEM((cols, rows), jnp.bfloat16),
+            pltpu.VMEM((cols, rows), jnp.bfloat16),
             pltpu.VMEM((cols, rows), jnp.float32),
         ],
         compiler_params=pltpu.CompilerParams(vmem_limit_bytes=48 * 1024 * 1024),
         cost_estimate=pl.CostEstimate(
-            flops=8 * rows * rows * cols * heads, bytes_accessed=14 * rows * cols, transcendentals=0
+            flops=10 * rows * rows * cols * heads, bytes_accessed=14 * rows * cols,
+            transcendentals=heads * rows * rows,
         ),
         name="window_grads",
-    )(probs, edge, own, cot_edge, cot)
+    )(bias, edge, own, cot_edge, cot)
 
 
 MESH = pl.DeviceIdType.MESH
 
 
-def exchange_kernel(n, group, heads, qkv_hbm, w_in_hbm, w_out_hbm, x_ref, grad_ref, gate_ref, route_ref, b_ref,
-                    got_ref, dact_ref, hidden_ref, gb_ref, edge_ref, cot_edge_ref, heads_ref, probs_ref,
-                    send_ref, place_t_ref, qkv_ref, w_in_ref, w_out_ref, q_t,
+def exchange_kernel(n, group, qkv_hbm, w_in_hbm, w_out_hbm, x_ref, grad_ref, gate_ref, route_ref, b_ref,
+                    got_out, dact_out, hidden_out, gb_ref, edge_ref, cot_edge_ref, heads_ref,
+                    got_ref, dact_ref, hidden_ref, send_ref, place_t_ref, w_in_ref, w_out_ref,
                     w_in_t, w_out_t, part_out, part_in, ret_out, ret_in,
                     send_sem, recv_sem, on_send, on_recv, part_send, part_recv, ret_send, ret_recv,
-                    edge_sem, cot_sem, own_sem, load_sem):
+                    edge_sem, cot_sem, own_sem, load_sem, keep_sem):
     loads = [
         pltpu.make_async_copy(src, dst, load_sem.at[i])
-        for i, (src, dst) in enumerate(((qkv_hbm, qkv_ref), (w_in_hbm, w_in_ref), (w_out_hbm, w_out_ref)))
+        for i, (src, dst) in enumerate(((w_in_hbm, w_in_ref), (w_out_hbm, w_out_ref)))
     ]
     for load in loads:
         load.start()
@@ -174,7 +142,7 @@
     capacity, half = ret_in.shape[1], ret_in.shape[2]
     rows = group * capacity
     lead = edge_ref.shape[1]
-    start = qkv_ref.shape[1] - lead
+    start = qkv_hbm.shape[1] - lead
     hidden_units = w_in_ref.shape[1]
     bits = n.bit_length() - 1
 
@@ -247,6 +215,7 @@
 
     back = {}
     parts = []
+    kept_out = []
     step = hidden_units // 4
     bias_sums = [0.0] * 4
     for g in range(n // group):
@@ -293,14 +262,13 @@
                 back[k] = remote(ret_out.at[partners[k]], ret_in.at[me], ret_send.at[k], ret_recv.at[k],
                                  (partners[k], core))
             back[k].start()
-        if g == 1:
-            edge.wait_recv()
-            window = qkv_ref.shape[1]
-            queries = jnp.concatenate([edge_ref[0], qkv_ref[0, : window - lead]], axis=0)
-            keys = jnp.concatenate([edge_ref[1], qkv_ref[1, : window - lead]], axis=0)
-            q_t[...] = queries.T
-            bias = jnp.where(me == 0, -1e30, 0.0).astype(jnp.float32)
-            window_probs(heads, lead, bias, keys, q_t, probs_ref)
+        for i, (src, dst) in enumerate(
+            ((got_ref.at[:, pl.ds(base, group)], got_out.at[:, pl.ds(base, group)]),
+             (dact_ref.at[span], dact_out.at[span]), (hidden_ref.at[span], hidden_out.at[span]))
+        ):
+            keep = pltpu.make_async_copy(src, dst, keep_sem.at[g, i])
+            keep.start()
+            kept_out.append(keep)
     for c in range(4):
         gb_ref[:, c * step : (c + 1) * step] = bias_sums[c]
 
@@ -327,11 +295,13 @@
             back[k].wait_send()
     for swap in parts:
         swap.wait_send()
-    edge.wait_send()
+    for keep in kept_out:
+        keep.wait()
+    edge.wait()
     cot.wait()
 
 
-def exchange(qkv, w_in, w_out, x, grad, gate, route, b_in, n, capacity, lead, heads):
+def exchange(qkv, w_in, w_out, x, grad, gate, route, b_in, n, capacity, lead):
     tokens, width = x.shape
     hidden_units = w_in.shape[1]
     half = qkv.shape[2]
@@ -342,7 +312,7 @@
     dma = pltpu.SemaphoreType.DMA
     shape = jax.ShapeDtypeStruct
     return pl.pallas_call(
-        functools.partial(exchange_kernel, n, group, heads),
+        functools.partial(exchange_kernel, n, group),
         out_shape=(
             shape((2, n, capacity, columns), bf16),
             shape((n * capacity, hidden_units), bf16),
@@ -351,17 +321,17 @@
             shape((3, lead, half), bf16),
             shape((lead, half), bf16),
             shape((tokens, half), bf16),
-            shape((heads, tokens, tokens), bf16),
         ),
         in_specs=[pl.BlockSpec(memory_space=pl.ANY)] * 3 + [vmem] * 5,
-        out_specs=[vmem] * 8,
+        out_specs=[pl.BlockSpec(memory_space=pl.ANY)] * 3 + [vmem] * 4,
         scratch_shapes=[
+            pltpu.VMEM((2, n, capacity, columns), bf16),
+            pltpu.VMEM((n * capacity, hidden_units), bf16),
+            pltpu.VMEM((n * capacity, hidden_units), bf16),
             pltpu.VMEM((n, capacity, columns), bf16),
             pltpu.VMEM((tokens, n * capacity), bf16),
-            pltpu.VMEM(qkv.shape, bf16),
             pltpu.VMEM(w_in.shape, bf16),
             pltpu.VMEM(w_out.shape, bf16),
-            pltpu.VMEM((half, tokens), bf16),
             pltpu.VMEM((hidden_units, width), bf16),
             pltpu.VMEM((width, hidden_units), bf16),
             pltpu.VMEM((n // group, group * capacity, half), bf16),
@@ -371,10 +341,10 @@
             dma((n,)), dma((n,)), dma((n,)), dma((n,)),
             dma((n // group,)), dma((n // group,)),
             dma((n,)), dma((n,)),
-            dma((2,)), dma((2,)), dma((2,)), dma((3,)),
+            dma((2,)), dma((2,)), dma((2,)), dma((2,)), dma((n // group, 3)),
         ],
         compiler_params=pltpu.CompilerParams(
-            collective_id=0, has_side_effects=True, vmem_limit_bytes=48 * 1024 * 1024
+            collective_id=0, has_side_effects=True, vmem_limit_bytes=60 * 1024 * 1024
         ),
         cost_estimate=pl.CostEstimate(
             flops=6 * n * capacity * width * hidden_units, bytes_accessed=16 * 1024 * 1024,
@@ -406,8 +376,8 @@
     lead = SHIFT * CELLS
     start = WIN_T * CELLS - lead
     if capacity % 16 == 0 and experts % 4 == 0 and experts & (experts - 1) == 0:
-        got, d_act, hidden, g_bias, qkv_edge, cot_edge, d_heads, probs = exchange(
-            qkv, w_in[0], w_out[0], moe_input, out_grad, gate[:, None], route, b_in, experts, capacity, lead, heads_here
+        got, d_act, hidden, g_bias, qkv_edge, cot_edge, d_heads = exchange(
+            qkv, w_in[0], w_out[0], moe_input, out_grad, gate[:, None], route, b_in, experts, capacity, lead
         )
         g_bias = g_bias[0]
         got = got.reshape(2, experts * capacity, 2 * half)
@@ -443,11 +413,10 @@
         d_moe = lax.dot_general(place, returned, (((0,), (0,)), ((), ())), preferred_element_type=jnp.float32)
         d_heads = (own_grad.astype(jnp.float32) + d_moe).astype(jnp.bfloat16)
         cot_edge = passed_along(d_heads[start:], "ex", 1)
-        bias = jnp.where(lax.axis_index("ex") == 0, -1e30, 0.0).astype(jnp.float32).reshape(1)
-        probs = separate_probs(bias, qkv_edge, qkv, heads_here)
+    bias = jnp.where(lax.axis_index("ex") == 0, -1e30, 0.0).astype(jnp.float32).reshape(1)
     pieces = []
     for part in range(2):
-        back, mine = window_grads(probs, qkv_edge, qkv, cot_edge, d_heads, part, 2)
+        back, mine = window_grads(bias, qkv_edge, qkv, cot_edge, d_heads, heads_here, part, 2)
         pieces.append(jnp.concatenate([mine, passed_along(back, "ex", -1)], axis=1))
     g_qkv = jnp.concatenate(pieces, axis=2)
     return (g_first[None], g_bias[None], g_second[None], g_qkv)

time: 96.9 us -> 88.4 us (0.912)
  local copies, waits for them, and re-layouts: 12.5 us -> 8.23 us
  Pallas kernels: 73.2 us -> 69 us
    pallas_call x1, Pallas kernels: 64 us -> 58.9 us  [exchange(): pl.pallas_call(functools.partial(exchange_kernel, n, group), out_shape=(s...]
    unnamed x22 -> x20, local copies, waits for them, and re-layouts: 11.4 us -> 6.43 us
  transfers between devices with their start and end apart: 2 -> 2, of which waited for: 0 -> 0; matrix products, arithmetic and copies ran while one was open for 6% -> 6% of each run, Pallas kernels for 5% -> 6%
where the time goes in v4:
time: 88.4 us; the launch traced here: 88.1 us
  Pallas kernels  69 us (78%)
  local copies, waits for them, and re-layouts  8.23 us (9%)
  matrix products  5.2 us (6%)
  starting transfers between devices  3.97 us (4%)
  other arithmetic  0.98 us (1%)
    pallas_call x1, Pallas kernels, exchange(): pl.pallas_call(functools.partial(exchange_kernel, n, group), out_shape=(s...  58.9 us
    pallas_call x2, Pallas kernels, window_grads(): pl.pallas_call(functools.partial(window_kernel, heads), grid=(1,), out_sh...  10.1 us
    unnamed x20, local copies, waits for them, and re-layouts  6.43 us
    ppermute x2, starting transfers between devices, passed_along(): return lax.ppermute(block, axis, route)  3.97 us
    dot_general x1, matrix products, weight_grads(): jnp.einsum('sf,sd->fd', hidden, s, preferred_element_type=jnp.float32)  2.61 us
    dot_general x1, matrix products, weight_grads(): jnp.einsum('sd,sf->df', x, d_act, preferred_element_type=jnp.float32)  2.59 us
  transfers between devices with their start and end apart: 2, of which 0 were waited for; matrix products, arithmetic and copies ran while one was open for 6% of the time, Pallas kernels for 6%

profile of v4, /device:TPU:0, one launch (start us, length us, event | category | flops | bytes accessed | tf_op | source)
XLA Modules:
  0.0 88.1 jit_solution(8815311565865012487)
XLA Ops:
  0.6 1.5 %copy.13.gate_ref = f32[512,1]{1,0:T(8,128)} copy(f32[512,1]{0,1:T(1,128)} %bitcast.14) | data formatting | bytes 4096 | tf_op jit(solution)/shard_map/broadcast_in_dim | solution.py:380
  2.2 1.5 %copy.14.route_ref = s32[512,1]{1,0:T(8,128)} copy(s32[512,1]{0,1:T(1,128)} %param.11) | data formatting | bytes 4096 | tf_op args[3]
  3.7 58.9 %exchange.1 = (bf16[2,16,64,512]{3,2,1,0:T(8,128)(2,1)}, bf16[1024,1024]{1,0:T(8,128)(2,1)}, bf16[1024,1024]{1,0:T(8,128)(2,1)}, f32[1,1024]{1,0:T(1,128)}, bf16...) custom-call(bf16[3,512,256]{2,1,0:T(8,128)(2,1)} %own_ref.3, ...), custom_call_target="tpu_custom_call" | custom-call | flops 3221225472 | bytes 16777216 | tf_op jit(solution)/shard_map/exchange/pallas_call | solution.py:314
  62.6 0.0 copy-done
  62.6 0.0 copy-start.1
  62.6 1.0 %copy-done.1 = bf16[3,256,256]{2,1,0:T(8,128)(2,1)S(1)} copy-done((bf16[3,256,256]{2,1,0:T(8,128)(2,1)S(1)}, bf16[3,256,256]{2,1,0:T(8,128)(2,1)}, u32[]{:S(2)}) %copy-start.1) | copy-done | bytes 393240
  63.6 0.9 %copy-done.3 = bf16[512,256]{1,0:T(8,128)(2,1)S(1)} copy-done((bf16[512,256]{1,0:T(8,128)(2,1)S(1)}, bf16[512,256]{1,0:T(8,128)(2,1)}, u32[]{:S(2)}) %copy-start.3) | copy-done | bytes 262168
  64.6 0.9 %copy-done.4 = bf16[256,256]{1,0:T(8,128)(2,1)S(1)} copy-done((bf16[256,256]{1,0:T(8,128)(2,1)S(1)}, bf16[256,256]{1,0:T(8,128)(2,1)}, u32[]{:S(2)}) %copy-start.4) | copy-done | bytes 131096
  65.5 5.0 %window_grads.2 = (bf16[3,256,128]{2,1,0:T(8,128)(2,1)S(1)}, bf16[3,256,128]{2,1,0:T(8,128)(2,1)S(1)}) custom-call(f32[1]{0:T(128)} %bitcast.7.bias_ref, bf16[3,256,256]{2,1,0:T(8,128)(2,1)S(1)} %copy-done.1, bf16[3,512,256]{2,1,0:T(8,128)(2,1)S(1)} %copy-done, bf16[256,256]{1,0:T(8,128)(2,1)S(1)} %copy-done.4, bf16[512,256]{1,0:T(8,128)(2,1)S(1)} %copy-done.3), custom_call_target="tpu_custom_call" | custom-call | flops 1342177280 | bytes 917504 | tf_op jit(solution)/shard_map/window_grads/pallas_call | solution.py:95
  70.5 0.0 copy-start.6
  70.5 1.7 %collective-permute-start = (bf16[3,256,128]{2,1,0:T(8,128)(2,1)S(1)}, bf16[3,256,128]{2,1,0:T(8,128)(2,1)S(1)}, u32[]{:S(2)}, u32[]{:S(2)}) collective-permute-start(bf16[3,256,128]{2,1,0:T(8,128)(2,1)S(1)} %get-tuple-element.23), channel_id=1, source_target_pairs={{2,0},{4,2},{6,4},{8,6},{10,8},{12,10},{14,12},{16,14},{18,16},{20... | collective-permute-start | bytes 589832 | tf_op jit(solution)/shard_map/ppermute | solution.py:20
  72.3 0.0 copy-done.2
  72.3 5.0 %window_grads.3 = (bf16[3,256,128]{2,1,0:T(8,128)(2,1)S(1)}, bf16[3,256,128]{2,1,0:T(8,128)(2,1)S(1)}) custom-call(f32[1]{0:T(128)} %bitcast.7.bias_ref, bf16[3,256,256]{2,1,0:T(8,128)(2,1)S(1)} %copy-done.2, bf16[3,512,256]{2,1,0:T(8,128)(2,1)S(1)} %copy-done, bf16[256,256]{1,0:T(8,128)(2,1)S(1)} %copy-done.4, bf16[512,256]{1,0:T(8,128)(2,1)S(1)} %copy-done.3), custom_call_target="tpu_custom_call" | custom-call | flops 1342177280 | bytes 917504 | tf_op jit(solution)/shard_map/window_grads/pallas_call | solution.py:95
  77.3 2.2 %collective-permute-start.1 = (bf16[3,256,128]{2,1,0:T(8,128)(2,1)S(1)}, bf16[3,256,128]{2,1,0:T(8,128)(2,1)S(1)}, u32[]{:S(2)}, u32[]{:S(2)}) collective-permute-start(bf16[3,256,128]{2,1,0:T(8,128)(2,1)S(1)} %get-tuple-element.25), channel_id=1, source_target_pairs={{2,0},{4,2},{6,4},{8,6},{10,8},{12,10},{14,12},{16,14},{18,16},{20... | collective-permute-start | bytes 589832 | tf_op jit(solution)/shard_map/ppermute | solution.py:20
  79.6 0.1 fusion.8
  79.7 0.0 copy-start.8
  79.7 0.1 fusion.9
  79.9 1.4 %copy-done.8 = bf16[1024,1024]{1,0:T(8,128)(2,1)S(1)} copy-done((bf16[1024,1024]{1,0:T(8,128)(2,1)S(1)}, bf16[1024,1024]{1,0:T(8,128)(2,1)}, u32[]{:S(2)}) %copy-start.8) | copy-done | bytes 2097176
  81.3 2.6 %convolution_bitcast_fusion = f32[1,1024,512]{2,1,0:T(8,128)} fusion(bf16[1024,1024]{1,0:T(8,128)(2,1)S(1)} %copy-done.8, bf16[1024,256]{1,0:T(8,128)(2,1)S(1)} %get-tuple-element.33, bf16[1024,256]{1,0:T(8,128)(2,1)S(1)} %get-tuple-element.28), kind=kOutput, calls=%fused_computation | convolution fusion | flops 1075838976 | bytes 5242880 | tf_op jit(solution)/shard_map/sf,sd->fd/dot_general | solution.py:359
  83.9 2.6 %convolution_bitcast_fusion.1 = f32[1,512,1024]{2,1,0:T(8,128)} fusion(bf16[1024,1024]{1,0:T(8,128)(2,1)S(1)} %copy-done.5, bf16[1024,256]{1,0:T(8,128)(2,1)S(1)} %get-tuple-element.32, bf16[1024,256]{1,0:T(8,128)(2,1)S(1)} %get-tuple-element.29), kind=kOutput, calls=%fused_computation.1 | convolution fusion | flops 1075838976 | bytes 5242880 | tf_op jit(solution)/shard_map/sd,sf->df/dot_general | solution.py:358
  86.5 0.0 collective-permute-done
  86.5 0.0 collective-permute-done.1
  86.5 1.0 %maximum_maximum_fusion = bf16[3,512,256]{2,1,0:T(8,128)(2,1)} fusion(bf16[3,256,128]{2,1,0:T(8,128)(2,1)S(1)} %collective-permute-done.1, bf16[3,256,128]{2,1,0:T(8,128)(2,1)S(1)} %get-tuple-element.24, bf16[3,256,128]{2,1,0:T(8,128)(2,1)S(1)} %collective-permute-done, bf16[3,256,128]{2,1,0:T(8,128)(2,1)S(1)} %get-tuple-element.22), kind=kLoop, calls=%fused_computation.8 | loop fusion | flops 3145728 | bytes 1572864 | tf_op jit(solution)/shard_map/concatenate | solution.py:421
  87.5 0.6 copy.16
  (9 shorter events, 0.0 us)
Async XLA Ops:
  3.7 58.9 %copy-start = (bf16[3,512,256]{2,1,0:T(8,128)(2,1)S(1)}, bf16[3,512,256]{2,1,0:T(8,128)(2,1)}, u32[]{:S(2)}) copy-start(bf16[3,512,256]{2,1,0:T(8,128)(2,1)} %own_ref.3) | copy-start | bytes 2359300
  62.6 1.0 %copy-start.1 = (bf16[3,256,256]{2,1,0:T(8,128)(2,1)S(1)}, bf16[3,256,256]{2,1,0:T(8,128)(2,1)}, u32[]{:S(2)}) copy-start(bf16[3,256,256]{2,1,0:T(8,128)(2,1)} %get-tuple-element.19.edge_ref) | copy-start | bytes 1179652
  63.6 0.9 %copy-start.3 = (bf16[512,256]{1,0:T(8,128)(2,1)S(1)}, bf16[512,256]{1,0:T(8,128)(2,1)}, u32[]{:S(2)}) copy-start(bf16[512,256]{1,0:T(8,128)(2,1)} %get-tuple-element.21.cot_ref) | copy-start | bytes 786436
  64.6 0.9 %copy-start.4 = (bf16[256,256]{1,0:T(8,128)(2,1)S(1)}, bf16[256,256]{1,0:T(8,128)(2,1)}, u32[]{:S(2)}) copy-start(bf16[256,256]{1,0:T(8,128)(2,1)} %get-tuple-element.20.cot_edge_ref) | copy-start | bytes 393220
  65.5 6.8 %copy-start.2 = (bf16[3,256,256]{2,1,0:T(8,128)(2,1)S(1)}, bf16[3,256,256]{2,1,0:T(8,128)(2,1)}, u32[]{:S(2)}) copy-start(bf16[3,256,256]{2,1,0:T(8,128)(2,1)} %get-tuple-element.19.edge_ref) | copy-start | bytes 1179652
  70.5 9.0 %copy-start.6 = (bf16[2,16,64,512]{3,2,1,0:T(8,128)(2,1)S(1)}, bf16[2,16,64,512]{3,2,1,0:T(8,128)(2,1)}, u32[]{:S(2)}) copy-start(bf16[2,16,64,512]{3,2,1,0:T(8,128)(2,1)} %get-tuple-element.15) | copy-start | bytes 6291460
  70.5 16.0 %collective-permute-start = (bf16[3,256,128]{2,1,0:T(8,128)(2,1)S(1)}, bf16[3,256,128]{2,1,0:T(8,128)(2,1)S(1)}, u32[]{:S(2)}, u32[]{:S(2)}) collective-permute-start(bf16[3,256,128]{2,1,0:T(8,128)(2,1)S(1)} %get-tuple-element.23), channel_id=1, source_target_pairs={{2,0},{4,2},{6,4},{8,6},{10,8},{12,10},{14,12},{16,14},{18,16},{20... | collective-permute-start | bytes 589832 | tf_op jit(solution)/shard_map/ppermute | solution.py:20
  77.3 9.2 %collective-permute-start.1 = (bf16[3,256,128]{2,1,0:T(8,128)(2,1)S(1)}, bf16[3,256,128]{2,1,0:T(8,128)(2,1)S(1)}, u32[]{:S(2)}, u32[]{:S(2)}) collective-permute-start(bf16[3,256,128]{2,1,0:T(8,128)(2,1)S(1)} %get-tuple-element.25), channel_id=1, source_target_pairs={{2,0},{4,2},{6,4},{8,6},{10,8},{12,10},{14,12},{16,14},{18,16},{20... | collective-permute-start | bytes 589832 | tf_op jit(solution)/shard_map/ppermute | solution.py:20
  79.7 1.6 %copy-start.8 = (bf16[1024,1024]{1,0:T(8,128)(2,1)S(1)}, bf16[1024,1024]{1,0:T(8,128)(2,1)}, u32[]{:S(2)}) copy-start(bf16[1024,1024]{1,0:T(8,128)(2,1)} %get-tuple-element.18) | copy-start | bytes 6291460
  81.3 2.6 %copy-start.5 = (bf16[1024,1024]{1,0:T(8,128)(2,1)S(1)}, bf16[1024,1024]{1,0:T(8,128)(2,1)}, u32[]{:S(2)}) copy-start(bf16[1024,1024]{1,0:T(8,128)(2,1)} %get-tuple-element.16) | copy-start | bytes 6291460
  83.9 3.6 %copy-start.7 = (f32[1,1024]{1,0:T(1,128)S(1)}, f32[1,1024]{1,0:T(1,128)}, u32[]{:S(2)}) copy-start(f32[1,1024]{1,0:T(1,128)} %get-tuple-element.39) | copy-start | bytes 12292

commit v5 on v4

--- a/solution.py
+++ b/solution.py
@@ -113,7 +113,7 @@
             pltpu.VMEM((cols, rows), jnp.bfloat16),
             pltpu.VMEM((cols, rows), jnp.float32),
         ],
-        compiler_params=pltpu.CompilerParams(vmem_limit_bytes=48 * 1024 * 1024),
+        compiler_params=pltpu.CompilerParams(vmem_limit_bytes=60 * 1024 * 1024),
         cost_estimate=pl.CostEstimate(
             flops=10 * rows * rows * cols * heads, bytes_accessed=14 * rows * cols,
             transcendentals=heads * rows * rows,
@@ -125,7 +125,7 @@
 MESH = pl.DeviceIdType.MESH
 
 
-def exchange_kernel(n, group, qkv_hbm, w_in_hbm, w_out_hbm, x_ref, grad_ref, gate_ref, route_ref, b_ref,
+def exchange_kernel(n, groups, qkv_hbm, w_in_hbm, w_out_hbm, x_ref, grad_ref, gate_ref, route_ref, b_ref,
                     got_out, dact_out, hidden_out, gb_ref, edge_ref, cot_edge_ref, heads_ref,
                     got_ref, dact_ref, hidden_ref, send_ref, place_t_ref, w_in_ref, w_out_ref,
                     w_in_t, w_out_t, part_out, part_in, ret_out, ret_in,
@@ -140,7 +140,6 @@
     me, core = lax.axis_index("ex"), lax.axis_index("hh")
     after, sibling = lax.rem(me + 1, n), 1 - core
     capacity, half = ret_in.shape[1], ret_in.shape[2]
-    rows = group * capacity
     lead = edge_ref.shape[1]
     start = qkv_hbm.shape[1] - lead
     hidden_units = w_in_ref.shape[1]
@@ -166,7 +165,8 @@
     edge.start()
 
     tokens, width = x_ref.shape
-    route = route_ref[...].astype(jnp.float32)
+    route = jnp.broadcast_to(route_ref[...].astype(jnp.float32), (8, tokens)).T[:, :1]
+    gate = jnp.broadcast_to(gate_ref[...], (8, tokens)).T[:, :1]
     expert = lax.broadcasted_iota(jnp.int32, (1, 128), 1).astype(jnp.float32)
     onehot = (route == expert).astype(jnp.float32)
     earlier = (
@@ -179,7 +179,7 @@
     place_t_ref[...] = place_t
     own_x = jnp.where(core == 0, x_ref[:, :half], x_ref[:, half:])
     own_grad = jnp.where(core == 0, grad_ref[:, :half], grad_ref[:, half:]).astype(jnp.float32)
-    own_s = (gate_ref[...] * own_grad).astype(jnp.bfloat16)
+    own_s = (gate * own_grad).astype(jnp.bfloat16)
     ready = jnp.dot(place_t.T, jnp.concatenate([own_x, own_s], axis=1), preferred_element_type=jnp.float32)
     send_ref[...] = ready.astype(jnp.bfloat16).reshape(n, capacity, 2 * half)
 
@@ -218,8 +218,8 @@
     kept_out = []
     step = hidden_units // 4
     bias_sums = [0.0] * 4
-    for g in range(n // group):
-        ks = range(g * group, (g + 1) * group)
+    for g, ks in enumerate(groups):
+        group, rows = len(ks), len(ks) * capacity
         for k in ks:
             if k == 0:
                 own.wait()
@@ -228,7 +228,7 @@
             passed[k].start()
         for k in ks:
             passed[k].wait_recv()
-        base = lax.div(partners[g * group], group) * group
+        base = lax.div(partners[ks[0]], group) * group
         low = got_ref[0, pl.ds(base, group)].reshape(rows, 2 * half)
         high = got_ref[1, pl.ds(base, group)].reshape(rows, 2 * half)
         x = jnp.concatenate([low[:, :half], high[:, :half]], axis=1)
@@ -248,12 +248,13 @@
             d_rows = more if d_rows is None else d_rows + more
         kept = jnp.where(core == 0, d_rows[:, :half], d_rows[:, half:])
         given = jnp.where(core == 0, d_rows[:, half:], d_rows[:, :half])
-        part_out[g] = given.astype(jnp.bfloat16)
-        swap = remote(part_out.at[g], part_in.at[g], part_send.at[g], part_recv.at[g], (me, sibling))
+        part_out[g, :rows] = given.astype(jnp.bfloat16)
+        halves = pl.ds(0, rows)
+        swap = remote(part_out.at[g, halves], part_in.at[g, halves], part_send.at[g], part_recv.at[g], (me, sibling))
         swap.start()
         parts.append(swap)
         swap.wait_recv()
-        total = (kept + part_in[g].astype(jnp.float32)).astype(jnp.bfloat16)
+        total = (kept + part_in[g, :rows].astype(jnp.float32)).astype(jnp.bfloat16)
         ret_out[pl.ds(base, group)] = total.reshape(group, capacity, half)
         for k in reversed(ks):
             if k == 0:
@@ -273,13 +274,14 @@
         gb_ref[:, c * step : (c + 1) * step] = bias_sums[c]
 
     total = jnp.where(core == 0, grad_ref[:, :half], grad_ref[:, half:]).astype(jnp.float32)
-    for g in range(n // group):
-        for k in range(g * group, (g + 1) * group):
+    for ks in groups:
+        group, rows = len(ks), len(ks) * capacity
+        for k in ks:
             if k == 0:
                 back[k].wait()
             else:
                 back[k].wait_recv()
-        base = lax.div(partners[g * group], group) * group
+        base = lax.div(partners[ks[0]], group) * group
         span = pl.ds(pl.multiple_of(base * capacity, rows), rows)
         total = total + jnp.dot(
             place_t_ref[:, span], ret_in[pl.ds(base, group)].reshape(rows, half),
@@ -306,13 +308,14 @@
     hidden_units = w_in.shape[1]
     half = qkv.shape[2]
     columns = 2 * half
-    group = 4
+    groups = [range(k, k + 4) for k in range(0, n // 2, 4)] + [range(k, k + 2) for k in range(n // 2, n, 2)]
+    count = len(groups)
     vmem = pl.BlockSpec(memory_space=pltpu.VMEM)
     bf16, f32 = jnp.bfloat16, jnp.float32
     dma = pltpu.SemaphoreType.DMA
     shape = jax.ShapeDtypeStruct
     return pl.pallas_call(
-        functools.partial(exchange_kernel, n, group),
+        functools.partial(exchange_kernel, n, groups),
         out_shape=(
             shape((2, n, capacity, columns), bf16),
             shape((n * capacity, hidden_units), bf16),
@@ -334,14 +337,14 @@
             pltpu.VMEM(w_out.shape, bf16),
             pltpu.VMEM((hidden_units, width), bf16),
             pltpu.VMEM((width, hidden_units), bf16),
-            pltpu.VMEM((n // group, group * capacity, half), bf16),
-            pltpu.VMEM((n // group, group * capacity, half), bf16),
+            pltpu.VMEM((count, 4 * capacity, half), bf16),
+            pltpu.VMEM((count, 4 * capacity, half), bf16),
             pltpu.VMEM((n, capacity, half), bf16),
             pltpu.VMEM((n, capacity, half), bf16),
             dma((n,)), dma((n,)), dma((n,)), dma((n,)),
-            dma((n // group,)), dma((n // group,)),
+            dma((count,)), dma((count,)),
             dma((n,)), dma((n,)),
-            dma((2,)), dma((2,)), dma((2,)), dma((2,)), dma((n // group, 3)),
+            dma((2,)), dma((2,)), dma((2,)), dma((2,)), dma((count, 3)),
         ],
         compiler_params=pltpu.CompilerParams(
             collective_id=0, has_side_effects=True, vmem_limit_bytes=60 * 1024 * 1024
@@ -375,9 +378,9 @@
     heads_here = HEADS // lax.axis_size("hh")
     lead = SHIFT * CELLS
     start = WIN_T * CELLS - lead
-    if capacity % 16 == 0 and experts % 4 == 0 and experts & (experts - 1) == 0:
+    if capacity % 16 == 0 and experts % 8 == 0 and experts & (experts - 1) == 0:
         got, d_act, hidden, g_bias, qkv_edge, cot_edge, d_heads = exchange(
-            qkv, w_in[0], w_out[0], moe_input, out_grad, gate[:, None], route, b_in, experts, capacity, lead
+            qkv, w_in[0], w_out[0], moe_input, out_grad, gate[None], route.reshape(1, tok_rows), b_in, experts, capacity, lead
         )
         g_bias = g_bias[0]
         got = got.reshape(2, experts * capacity, 2 * half)

time: 88.4 us -> 89.2 us (level)
  Pallas kernels: 69 us -> 76.4 us
  local copies, waits for them, and re-layouts: 8.23 us -> 2.41 us
    unnamed x20 -> x13, local copies, waits for them, and re-layouts: 6.43 us -> 2.06 us
    pallas_call x1, Pallas kernels: 58.9 us -> 62.8 us  [exchange(): pl.pallas_call(functools.partial(exchange_kernel, n, groups), out_shape=(...]
    pallas_call x2, Pallas kernels: 10.1 us -> 13.7 us  [window_grads(): pl.pallas_call(functools.partial(window_kernel, heads), grid=(1,), out_sh...]
    broadcast_in_dim x1 -> x0, local copies, waits for them, and re-layouts: 1.54 us -> none  [local(): gate[:, None]]
  transfers between devices with their start and end apart: 2 -> 2, of which waited for: 0 -> 0; matrix products, arithmetic and copies ran while one was open for 6% -> 6% of each run, Pallas kernels for 6% -> 8%
where the time goes in v5:
time: 89.2 us; the launch traced here: 88.9 us
  Pallas kernels  76.4 us (86%)
  matrix products  5.19 us (6%)
  starting transfers between devices  3.23 us (4%)
  local copies, waits for them, and re-layouts  2.41 us (3%)
  other arithmetic  0.98 us (1%)
    pallas_call x1, Pallas kernels, exchange(): pl.pallas_call(functools.partial(exchange_kernel, n, groups), out_shape=(...  62.8 us
    pallas_call x2, Pallas kernels, window_grads(): pl.pallas_call(functools.partial(window_kernel, heads), grid=(1,), out_sh...  13.7 us
    ppermute x2, starting transfers between devices, passed_along(): return lax.ppermute(block, axis, route)  3.23 us
    dot_general x1, matrix products, weight_grads(): jnp.einsum('sf,sd->fd', hidden, s, preferred_element_type=jnp.float32)  2.6 us
    dot_general x1, matrix products, weight_grads(): jnp.einsum('sd,sf->df', x, d_act, preferred_element_type=jnp.float32)  2.59 us
    unnamed x13, local copies, waits for them, and re-layouts  2.06 us
  transfers between devices with their start and end apart: 2, of which 0 were waited for; matrix products, arithmetic and copies ran while one was open for 6% of the time, Pallas kernels for 8%

profile of v5, /device:TPU:0, one launch (start us, length us, event | category | flops | bytes accessed | tf_op | source)
XLA Modules:
  0.0 88.9 jit_solution(12598967695509330849)
XLA Ops:
  0.6 62.8 %exchange.1 = (bf16[2,16,64,512]{3,2,1,0:T(8,128)(2,1)}, bf16[1024,1024]{1,0:T(8,128)(2,1)}, bf16[1024,1024]{1,0:T(8,128)(2,1)}, f32[1,1024]{1,0:T(1,128)}, bf16...) custom-call(bf16[3,512,256]{2,1,0:T(8,128)(2,1)} %own_ref.3, ...), custom_call_target="tpu_custom_call" | custom-call | flops 3221225472 | bytes 16777216 | tf_op jit(solution)/shard_map/exchange/pallas_call | solution.py:317
  63.4 6.8 %window_grads.2 = (bf16[3,256,128]{2,1,0:T(8,128)(2,1)}, bf16[3,256,128]{2,1,0:T(8,128)(2,1)}) custom-call(f32[1]{0:T(128)} %bitcast.8.bias_ref, bf16[3,256,256]{2,1,0:T(8,128)(2,1)} %get-tuple-element.19.edge_ref, bf16[3,512,256]{2,1,0:T(8,128)(2,1)} %own_ref.3, bf16[256,256]{1,0:T(8,128)(2,1)} %get-tuple-element.20.cot_edge_ref, ...), custom_call_target="tpu_custom_call" | custom-call | flops 1342177280 | bytes 917504 | tf_op jit(solution)/shard_map/window_grads/pallas_call | solution.py:95
  70.2 0.0 copy-start.1
  70.3 1.1 %collective-permute-start = (bf16[3,256,128]{2,1,0:T(8,128)(2,1)}, bf16[3,256,128]{2,1,0:T(8,128)(2,1)S(1)}, u32[]{:S(2)}, u32[]{:S(2)}) collective-permute-start(bf16[3,256,128]{2,1,0:T(8,128)(2,1)} %get-tuple-element.23), channel_id=1, source_target_pairs={{2,0},{4,2},{6,4},{8,6},{10,8},{12,10},{14,12},{16,14},{18,16},{20... | collective-permute-start | bytes 589832 | tf_op jit(solution)/shard_map/ppermute | solution.py:20
  71.4 6.8 %window_grads.3 = (bf16[3,256,128]{2,1,0:T(8,128)(2,1)}, bf16[3,256,128]{2,1,0:T(8,128)(2,1)}) custom-call(f32[1]{0:T(128)} %bitcast.8.bias_ref, bf16[3,256,256]{2,1,0:T(8,128)(2,1)} %get-tuple-element.19.edge_ref, bf16[3,512,256]{2,1,0:T(8,128)(2,1)} %own_ref.3, bf16[256,256]{1,0:T(8,128)(2,1)} %get-tuple-element.20.cot_edge_ref, ...), custom_call_target="tpu_custom_call" | custom-call | flops 1342177280 | bytes 917504 | tf_op jit(solution)/shard_map/window_grads/pallas_call | solution.py:95
  78.2 2.1 %collective-permute-start.1 = (bf16[3,256,128]{2,1,0:T(8,128)(2,1)}, bf16[3,256,128]{2,1,0:T(8,128)(2,1)S(1)}, u32[]{:S(2)}, u32[]{:S(2)}) collective-permute-start(bf16[3,256,128]{2,1,0:T(8,128)(2,1)} %get-tuple-element.25), channel_id=1, source_target_pairs={{2,0},{4,2},{6,4},{8,6},{10,8},{12,10},{14,12},{16,14},{18,16},{20... | collective-permute-start | bytes 589832 | tf_op jit(solution)/shard_map/ppermute | solution.py:20
  80.3 0.0 copy-done.1
  80.3 0.2 fusion.8
  80.5 0.0 copy-start.5
  80.6 0.1 fusion.9
  80.7 1.4 %copy-done.5 = bf16[1024,1024]{1,0:T(8,128)(2,1)S(1)} copy-done((bf16[1024,1024]{1,0:T(8,128)(2,1)S(1)}, bf16[1024,1024]{1,0:T(8,128)(2,1)}, u32[]{:S(2)}) %copy-start.5) | copy-done | bytes 2097176
  82.1 2.6 %convolution_bitcast_fusion = f32[1,1024,512]{2,1,0:T(8,128)} fusion(bf16[1024,1024]{1,0:T(8,128)(2,1)S(1)} %copy-done.5, bf16[1024,256]{1,0:T(8,128)(2,1)S(1)} %get-tuple-element.33, bf16[1024,256]{1,0:T(8,128)(2,1)S(1)} %get-tuple-element.28), kind=kOutput, calls=%fused_computation | convolution fusion | flops 1075838976 | bytes 5242880 | tf_op jit(solution)/shard_map/sf,sd->fd/dot_general | solution.py:362
  84.7 0.0 copy-done
  84.8 0.0 copy-start.2
  84.8 0.0 copy-start.3
  84.8 0.0 copy-start.4
  84.8 2.6 %convolution_bitcast_fusion.1 = f32[1,512,1024]{2,1,0:T(8,128)} fusion(bf16[1024,1024]{1,0:T(8,128)(2,1)S(1)} %copy-done, bf16[1024,256]{1,0:T(8,128)(2,1)S(1)} %get-tuple-element.32, bf16[1024,256]{1,0:T(8,128)(2,1)S(1)} %get-tuple-element.29), kind=kOutput, calls=%fused_computation.1 | convolution fusion | flops 1075838976 | bytes 5242880 | tf_op jit(solution)/shard_map/sd,sf->df/dot_general | solution.py:361
  87.3 0.0 collective-permute-done
  87.4 0.0 collective-permute-done.1
  87.4 0.0 copy-done.2
  87.4 0.0 copy-done.3
  87.4 1.0 %maximum_maximum_fusion = bf16[3,512,256]{2,1,0:T(8,128)(2,1)} fusion(bf16[3,256,128]{2,1,0:T(8,128)(2,1)S(1)} %collective-permute-done.1, bf16[3,256,128]{2,1,0:T(8,128)(2,1)S(1)} %copy-done.3, bf16[3,256,128]{2,1,0:T(8,128)(2,1)S(1)} %collective-permute-done, bf16[3,256,128]{2,1,0:T(8,128)(2,1)S(1)} %copy-done.2), kind=kLoop, calls=%fused_computation.8 | loop fusion | flops 3145728 | bytes 1572864 | tf_op jit(solution)/shard_map/concatenate | solution.py:424
  88.4 0.0 copy-done.4
  88.4 0.6 copy.13
  (1 shorter events, 0.0 us)
Async XLA Ops:
  70.2 10.1 %copy-start.1 = (bf16[2,16,64,512]{3,2,1,0:T(8,128)(2,1)S(1)}, bf16[2,16,64,512]{3,2,1,0:T(8,128)(2,1)}, u32[]{:S(2)}) copy-start(bf16[2,16,64,512]{3,2,1,0:T(8,128)(2,1)} %get-tuple-element.15) | copy-start | bytes 6291460
  70.3 17.1 %collective-permute-start = (bf16[3,256,128]{2,1,0:T(8,128)(2,1)}, bf16[3,256,128]{2,1,0:T(8,128)(2,1)S(1)}, u32[]{:S(2)}, u32[]{:S(2)}) collective-permute-start(bf16[3,256,128]{2,1,0:T(8,128)(2,1)} %get-tuple-element.23), channel_id=1, source_target_pairs={{2,0},{4,2},{6,4},{8,6},{10,8},{12,10},{14,12},{16,14},{18,16},{20... | collective-permute-start | bytes 589832 | tf_op jit(solution)/shard_map/ppermute | solution.py:20
  78.2 9.2 %collective-permute-start.1 = (bf16[3,256,128]{2,1,0:T(8,128)(2,1)}, bf16[3,256,128]{2,1,0:T(8,128)(2,1)S(1)}, u32[]{:S(2)}, u32[]{:S(2)}) collective-permute-start(bf16[3,256,128]{2,1,0:T(8,128)(2,1)} %get-tuple-element.25), channel_id=1, source_target_pairs={{2,0},{4,2},{6,4},{8,6},{10,8},{12,10},{14,12},{16,14},{18,16},{20... | collective-permute-start | bytes 589832 | tf_op jit(solution)/shard_map/ppermute | solution.py:20
  80.5 1.6 %copy-start.5 = (bf16[1024,1024]{1,0:T(8,128)(2,1)S(1)}, bf16[1024,1024]{1,0:T(8,128)(2,1)}, u32[]{:S(2)}) copy-start(bf16[1024,1024]{1,0:T(8,128)(2,1)} %get-tuple-element.18) | copy-start | bytes 6291460
  82.1 2.6 %copy-start = (bf16[1024,1024]{1,0:T(8,128)(2,1)S(1)}, bf16[1024,1024]{1,0:T(8,128)(2,1)}, u32[]{:S(2)}) copy-start(bf16[1024,1024]{1,0:T(8,128)(2,1)} %get-tuple-element.16) | copy-start | bytes 6291460
  84.8 2.6 %copy-start.2 = (bf16[3,256,128]{2,1,0:T(8,128)(2,1)S(1)}, bf16[3,256,128]{2,1,0:T(8,128)(2,1)}, u32[]{:S(2)}) copy-start(bf16[3,256,128]{2,1,0:T(8,128)(2,1)} %get-tuple-element.22) | copy-start | bytes 589828
  84.8 2.6 %copy-start.3 = (bf16[3,256,128]{2,1,0:T(8,128)(2,1)S(1)}, bf16[3,256,128]{2,1,0:T(8,128)(2,1)}, u32[]{:S(2)}) copy-start(bf16[3,256,128]{2,1,0:T(8,128)(2,1)} %get-tuple-element.24) | copy-start | bytes 589828
  84.8 3.6 %copy-start.4 = (f32[1,1024]{1,0:T(1,128)S(1)}, f32[1,1024]{1,0:T(1,128)}, u32[]{:S(2)}) copy-start(f32[1,1024]{1,0:T(1,128)} %get-tuple-element.39) | copy-start | bytes 12292
